TPU v7x, 32 devices: a whole 2x2x4 slice. The times are simulated.
32 devices in a mesh: dp: 8 (over y, x, core), rows: 4 (over z).
Axes of the slice: x: 2, y: 2, z: 4, core: 2. Of those that a mesh axis runs over, the one named last changes fastest.
Arguments:
- inputs: float32 [64, 8, 44, 512], P('rows', 'dp'), may hold values from -60 to 60
- image_ids: int32 [64, 8, 44], P('rows', 'dp'), may hold values from -1 to 6, as said below
- first_norm_gain: float32 [512], replicated, may hold values from 0.5 to 1.5
- first_norm_bias: float32 [512], replicated, may hold values from -0.5 to 0.5
- point_one: float32 [512, 512], replicated, may hold values from -0.25 to 0.25
- kernel_big: float32 [27, 27, 512], replicated, may hold values from -0.21875 to 0.21875
- kernel_small: float32 [5, 5, 512], replicated, may hold values from -1.25 to 1.25
- second_norm_gain: float32 [512], replicated, may hold values from 0.5 to 1.5
- second_norm_bias: float32 [512], replicated, may hold values from -0.5 to 0.5
- point_two: float32 [512, 512], replicated, may hold values from -0.25 to 0.25
- feedforward_norm_gain: float32 [512], replicated, may hold values from 0.5 to 1.5
- feedforward_norm_bias: float32 [512], replicated, may hold values from -0.5 to 0.5
- w_up: float32 [512, 2048], P(None, 'rows'), may hold values from -0.25 to 0.25
- w_down: float32 [2048, 512], P('rows'), may hold values from -0.125 to 0.125
- out_grad: float32 [64, 8, 44, 512], P('rows', 'dp'), may hold values from -6 to 6
Outputs:
- output: float32 [64, 8, 44, 512], P('rows', 'dp')
- grad_input: float32 [64, 8, 44, 512], P('rows', 'dp')
- grad_gain_one: float32 [512], replicated
- grad_bias_one: float32 [512], replicated
- grad_point_one: float32 [512, 512], replicated
- grad_kernel_big: float32 [27, 27, 512], replicated
- grad_kernel_small: float32 [5, 5, 512], replicated
- grad_gain_two: float32 [512], replicated
- grad_bias_two: float32 [512], replicated
- grad_point_two: float32 [512, 512], replicated
- grad_gain_three: float32 [512], replicated
- grad_bias_three: float32 [512], replicated
- grad_w_up: float32 [512, 2048], P(None, 'rows')
- grad_w_down: float32 [2048, 512], P('rows')
Inputs may be any that keep to these rules, and one draw needn't show every extreme that they name: `image_ids`: each canvas packs three square maps of sides 24, 24 and 14 stacked in its left columns and four 14 x 14 maps stacked to their right; ids 0 to 2 name the first three, 3 to 6 the others; -1 marks unused pixels.
All inputs are finite; a program needn't handle non-finite values.
Results may differ from a plain program's by a relative error of at most 0.0003.
Values sent between devices are 32-bit elements; how exact they have to be, the bound alone decides.
A program may use at most 192 MiB of HBM per device.

v0:
```python
import jax
import jax.numpy as jnp
from jax import lax
from jax.sharding import PartitionSpec as P

EPSILON = 1e-05
HIGHEST = lax.Precision.HIGHEST


def with_halo(cells, sides, width):
    for axis, dim in sides:
        count = lax.axis_size(axis)
        ends = count - 1
        head = lax.slice_in_dim(cells, 0, width, axis=dim)
        tail = lax.slice_in_dim(cells, cells.shape[dim] - width, cells.shape[dim], axis=dim)
        cells = jnp.concatenate(
            [
                lax.ppermute(tail, axis, [(i, (i + 1) % count) for i in range(ends)]),
                cells,
                lax.ppermute(head, axis, [((i + 1) % count, i) for i in range(ends)]),
            ],
            axis=dim,
        )
    return cells


def product(left, right):
    return jnp.dot(left, right, precision=HIGHEST, preferred_element_type=jnp.float32)


def contract(left, right):
    return jnp.tensordot(left, right, axes=((0, 1, 2), (0, 1, 2)), precision=HIGHEST)


def row_group():
    return 3


def depthwise(padded, id_padded, image_ids, kernel):
    row_count = image_ids.shape[0]
    width_count = image_ids.shape[2]
    kernel_span = kernel.shape[0]
    group = row_group()

    def depthwise_row_step(running, offset):
        weights = lax.dynamic_slice_in_dim(kernel, offset, group, 0)
        for inner in range(group):
            row_slab = lax.dynamic_slice_in_dim(padded, offset + inner, row_count, 0)
            id_slab = lax.dynamic_slice_in_dim(id_padded, offset + inner, row_count, 0)
            for column in range(kernel_span):
                same_image = (id_slab[:, :, column : column + width_count] == image_ids)[..., None]
                running = (
                    running
                    + jnp.where(same_image, row_slab[:, :, column : column + width_count], 0.0)
                    * weights[inner, column]
                )
        return (running, None)

    start_sum = jnp.zeros(image_ids.shape + (kernel.shape[2],), jnp.float32)
    offsets = jnp.arange(0, kernel_span, group, dtype=jnp.int32)
    result, ignored_value = lax.scan(depthwise_row_step, start_sum, offsets)
    return result


def kernel_grad(padded, id_padded, image_ids, upstream, kernel_span):
    row_count = image_ids.shape[0]
    width_count = image_ids.shape[2]
    group = row_group()

    def kernel_row_step(carried, offset):
        group_rows = []
        for inner in range(group):
            row_slab = lax.dynamic_slice_in_dim(padded, offset + inner, row_count, 0)
            id_slab = lax.dynamic_slice_in_dim(id_padded, offset + inner, row_count, 0)
            kernel_cells = []
            for column in range(kernel_span):
                same_image = (id_slab[:, :, column : column + width_count] == image_ids)[..., None]
                kernel_cells.append(
                    jnp.sum(
                        jnp.where(same_image, row_slab[:, :, column : column + width_count], 0.0)
                        * upstream,
                        axis=(0, 1, 2),
                    )
                )
            group_rows.append(jnp.stack(kernel_cells))
        return (carried, jnp.stack(group_rows))

    offsets = jnp.arange(0, kernel_span, group, dtype=jnp.int32)
    ignored_value, kernel_rows = lax.scan(kernel_row_step, jnp.zeros((), jnp.float32), offsets)
    return kernel_rows.reshape((kernel_span, kernel_span, upstream.shape[3]))


def shards(
    inputs,
    image_ids,
    first_norm_gain,
    first_norm_bias,
    point_one,
    kernel_big,
    kernel_small,
    second_norm_gain,
    second_norm_bias,
    point_two,
    feedforward_norm_gain,
    feedforward_norm_bias,
    w_up,
    w_down,
    out_grad,
):
    valid_mask = (image_ids >= 0).astype(jnp.float32)[..., None]
    kernel_span = kernel_big.shape[0]
    kernel_reach = kernel_span // 2
    small_span = kernel_small.shape[0]
    small_start = kernel_reach - small_span // 2

    def apply_layer_norm(field, gain_vec, bias_vec):
        valid_field = field * valid_mask
        total_sum, square_sum, canvas_pixel_count = lax.psum(
            (
                jnp.sum(valid_field, axis=(0, 1, 2)),
                jnp.sum(valid_field * field, axis=(0, 1, 2)),
                jnp.sum(valid_mask),
            ),
            ("dp", "rows"),
        )
        channel_mean = total_sum / canvas_pixel_count
        inv_scale = lax.rsqrt(
            square_sum / canvas_pixel_count - channel_mean * channel_mean + EPSILON
        )
        normed = (field - channel_mean) * inv_scale
        return ((normed * gain_vec + bias_vec) * valid_mask, normed, inv_scale, canvas_pixel_count)

    def denormalize(upstream, normed, inv_scale, gain_vec, canvas_pixel_count):
        masked = upstream * valid_mask
        grad_bias_vec, grad_gain_vec = lax.psum(
            (jnp.sum(masked, axis=(0, 1, 2)), jnp.sum(masked * normed, axis=(0, 1, 2))),
            ("dp", "rows"),
        )
        grad_field = (
            valid_mask
            * gain_vec
            * inv_scale
            * (
                masked
                - grad_bias_vec / canvas_pixel_count
                - normed * grad_gain_vec / canvas_pixel_count
            )
        )
        return (grad_field, grad_gain_vec, grad_bias_vec)

    def pad_columns(field, fill_value):
        pad_widths = [(0, 0)] * field.ndim
        pad_widths[2] = (kernel_reach, kernel_reach)
        return jnp.pad(field, pad_widths, constant_values=fill_value)

    id_padded = pad_columns(with_halo(image_ids, (("rows", 0),), kernel_reach), -2)
    first_normed_output, first_centered_input, first_inverse_scale, canvas_pixel_count = (
        apply_layer_norm(inputs, first_norm_gain, first_norm_bias)
    )
    hidden_one = product(first_normed_output, point_one)
    act_one, gelu_back_one = jax.vjp(jax.nn.gelu, hidden_one)
    kernel = kernel_big + jnp.pad(
        kernel_small, ((small_start, small_start), (small_start, small_start), (0, 0))
    )
    act_padded = pad_columns(with_halo(act_one, (("rows", 0),), kernel_reach), 0.0)
    depthwise_output = depthwise(act_padded, id_padded, image_ids, kernel) * valid_mask
    second_normed_output, second_centered_input, second_inverse_scale, ignored_value = (
        apply_layer_norm(depthwise_output, second_norm_gain, second_norm_bias)
    )
    act_two, gelu_back_two = jax.vjp(jax.nn.gelu, second_normed_output)
    mixed_output = inputs + product(act_two, point_two)
    third_normed_output, third_centered_input, third_inverse_scale, ignored_value = (
        apply_layer_norm(mixed_output, feedforward_norm_gain, feedforward_norm_bias)
    )
    gathered = lax.all_gather(third_normed_output, "rows", axis=0, tiled=True)
    pre_act = product(gathered, w_up)
    hidden_act, gelu_back_ffn = jax.vjp(jax.nn.gelu, pre_act)
    output = mixed_output + lax.psum_scatter(
        product(hidden_act, w_down), "rows", scatter_dimension=0, tiled=True
    )
    grad_gathered = lax.all_gather(out_grad, "rows", axis=0, tiled=True)
    grad_w_down = contract(hidden_act, grad_gathered)
    grad_pre = gelu_back_ffn(product(grad_gathered, w_down.T))[0]
    grad_w_up = contract(gathered, grad_pre)
    third_normed_gradient = lax.psum_scatter(
        product(grad_pre, w_up.T), "rows", scatter_dimension=0, tiled=True
    )
    grad_w_up, grad_w_down = lax.psum((grad_w_up, grad_w_down), "dp")
    grad_mixed_norm, grad_gain_three, grad_bias_three = denormalize(
        third_normed_gradient,
        third_centered_input,
        third_inverse_scale,
        feedforward_norm_gain,
        canvas_pixel_count,
    )
    grad_mixed = out_grad + grad_mixed_norm
    grad_point_two = contract(act_two, grad_mixed)
    second_normed_gradient = gelu_back_two(product(grad_mixed, point_two.T))[0]
    grad_conv, grad_gain_two, grad_bias_two = denormalize(
        second_normed_gradient,
        second_centered_input,
        second_inverse_scale,
        second_norm_gain,
        canvas_pixel_count,
    )
    grad_padded = pad_columns(with_halo(grad_conv, (("rows", 0),), kernel_reach), 0.0)
    grad_act = depthwise(grad_padded, id_padded, image_ids, kernel[::-1, ::-1])
    grad_kernel = kernel_grad(act_padded, id_padded, image_ids, grad_conv, kernel_span)
    grad_hidden_one = gelu_back_one(grad_act)[0]
    grad_point_one = contract(first_normed_output, grad_hidden_one)
    first_normed_gradient = product(grad_hidden_one, point_one.T)
    grad_input_norm, grad_gain_one, grad_bias_one = denormalize(
        first_normed_gradient,
        first_centered_input,
        first_inverse_scale,
        first_norm_gain,
        canvas_pixel_count,
    )
    grad_input = grad_mixed + grad_input_norm
    grad_small_local = grad_kernel[
        small_start : small_start + small_span, small_start : small_start + small_span
    ]
    grad_point_one, grad_point_two, grad_kernel, grad_small = lax.psum(
        (grad_point_one, grad_point_two, grad_kernel, grad_small_local), ("dp", "rows")
    )
    return (
        output,
        grad_input,
        grad_gain_one,
        grad_bias_one,
        grad_point_one,
        grad_kernel,
        grad_small,
        grad_gain_two,
        grad_bias_two,
        grad_point_two,
        grad_gain_three,
        grad_bias_three,
        grad_w_up,
        grad_w_down,
    )


def solution(mesh):
    placed = (
        P("rows", "dp", None, None),
        P("rows", "dp", None),
        P(),
        P(),
        P(),
        P(),
        P(),
        P(),
        P(),
        P(),
        P(),
        P(),
        P(None, "rows"),
        P("rows", None),
        P("rows", "dp", None, None),
    )
    return jax.shard_map(
        shards,
        mesh=mesh,
        in_specs=placed,
        out_specs=(
            P("rows", "dp", None, None),
            P("rows", "dp", None, None),
            P(),
            P(),
            P(),
            P(),
            P(),
            P(),
            P(),
            P(),
            P(),
            P(),
            P(None, "rows"),
            P("rows", None),
        ),
        check_vma=False,
    )
```

profile of v0, /device:TPU:0, one launch (start us, length us, event | category | flops | bytes accessed | tf_op | source)
XLA Modules:
  0.0 2891.4 jit_solution(13988592666331907792)
XLA Ops:
  11.1 42.3 %all-reduce.9 = (f32[512]{0:T(512)S(1)}, f32[]{:T(128)}, f32[512]{0:T(512)S(1)}) all-reduce(f32[512]{0:T(512)S(1)} %get-tuple-element.529, f32[]{:T(128)} %fusion.1085, f32[512]{0:T(512)S(1)} %get-tuple-element.528), channel_id=1, replica_groups=mesh['dp'=8,'rows'=4] {'dp','rows'}, use_global_device_ids=true, to_apply=%region_5.6 | all-reduce | flops 1025 | bytes 8200 | tf_op jit(solution)/shard_map/psum | solution.py:118
  78.0 12.8 collective-permute-done
  104.6 788.0 %while.39 = (s32[]{:T(128)}, f32[16,1,44,512]{3,2,1,0:T(8,128)S(1)}, s32[9]{0:T(128)S(1)}, s32[42,1,70]{2,0,1:T(8,128)S(1)}, s32[16,1,44]{2,0,1:T(8,128)S(1)}, /...) while((s32[]{:T(128)}, ...), condition=%wide.region_7.8_spmd.clone, body=%wide.region_6.7_spmd.clone.sunk | while | flops 88006376 | bytes 120518344 | solution.py:61
  115.8 78.0 %fusion.1134 = f32[16,1,44,512]{3,2,1,0:T(8,128)S(1)} fusion(f32[42,1,70,512]{3,2,1,0:T(8,128)} %get-tuple-element.2202, s32[]{:T(128)S(6)} %select_n.3518, s32[]{:T(128)S(6)} %add.3161, s32[]{:T(128)S(6)} %add.3162, s32[]{:T(128)S(6)} %add.3163, s32[]{:T(128)S(6)} %add.3164, s32[]{:T(128)S(6)} %add.3165, s32[]{:T(128)S(6)} %add.3166, ...), kind=kLoop, calls=%fused_computation.490.clone.1 | loop fusion | flops 87949312 | bytes 119891768 | tf_op jit(solution)/shard_map/while/body/eval_jaxpr/add | solution.py:53
  205.0 77.3 %fusion.1134 = f32[16,1,44,512]{3,2,1,0:T(8,128)S(1)} fusion(f32[42,1,70,512]{3,2,1,0:T(8,128)} %get-tuple-element.2202, s32[]{:T(128)S(6)} %select_n.3518, s32[]{:T(128)S(6)} %add.3161, s32[]{:T(128)S(6)} %add.3162, s32[]{:T(128)S(6)} %add.3163, s32[]{:T(128)S(6)} %add.3164, s32[]{:T(128)S(6)} %add.3165, s32[]{:T(128)S(6)} %add.3166, ...), kind=kLoop, calls=%fused_computation.490.clone.1 | loop fusion | flops 87949312 | bytes 119891768 | tf_op jit(solution)/shard_map/while/body/eval_jaxpr/add | solution.py:53
  293.5 76.6 %fusion.1134 = f32[16,1,44,512]{3,2,1,0:T(8,128)S(1)} fusion(f32[42,1,70,512]{3,2,1,0:T(8,128)} %get-tuple-element.2202, s32[]{:T(128)S(6)} %select_n.3518, s32[]{:T(128)S(6)} %add.3161, s32[]{:T(128)S(6)} %add.3162, s32[]{:T(128)S(6)} %add.3163, s32[]{:T(128)S(6)} %add.3164, s32[]{:T(128)S(6)} %add.3165, s32[]{:T(128)S(6)} %add.3166, ...), kind=kLoop, calls=%fused_computation.490.clone.1 | loop fusion | flops 87949312 | bytes 119891768 | tf_op jit(solution)/shard_map/while/body/eval_jaxpr/add | solution.py:53
  381.5 78.1 %fusion.1134 = f32[16,1,44,512]{3,2,1,0:T(8,128)S(1)} fusion(f32[42,1,70,512]{3,2,1,0:T(8,128)} %get-tuple-element.2202, s32[]{:T(128)S(6)} %select_n.3518, s32[]{:T(128)S(6)} %add.3161, s32[]{:T(128)S(6)} %add.3162, s32[]{:T(128)S(6)} %add.3163, s32[]{:T(128)S(6)} %add.3164, s32[]{:T(128)S(6)} %add.3165, s32[]{:T(128)S(6)} %add.3166, ...), kind=kLoop, calls=%fused_computation.490.clone.1 | loop fusion | flops 87949312 | bytes 119891768 | tf_op jit(solution)/shard_map/while/body/eval_jaxpr/add | solution.py:53
  470.9 75.4 %fusion.1134 = f32[16,1,44,512]{3,2,1,0:T(8,128)S(1)} fusion(f32[42,1,70,512]{3,2,1,0:T(8,128)} %get-tuple-element.2202, s32[]{:T(128)S(6)} %select_n.3518, s32[]{:T(128)S(6)} %add.3161, s32[]{:T(128)S(6)} %add.3162, s32[]{:T(128)S(6)} %add.3163, s32[]{:T(128)S(6)} %add.3164, s32[]{:T(128)S(6)} %add.3165, s32[]{:T(128)S(6)} %add.3166, ...), kind=kLoop, calls=%fused_computation.490.clone.1 | loop fusion | flops 87949312 | bytes 119891768 | tf_op jit(solution)/shard_map/while/body/eval_jaxpr/add | solution.py:53
  557.5 78.4 %fusion.1134 = f32[16,1,44,512]{3,2,1,0:T(8,128)S(1)} fusion(f32[42,1,70,512]{3,2,1,0:T(8,128)} %get-tuple-element.2202, s32[]{:T(128)S(6)} %select_n.3518, s32[]{:T(128)S(6)} %add.3161, s32[]{:T(128)S(6)} %add.3162, s32[]{:T(128)S(6)} %add.3163, s32[]{:T(128)S(6)} %add.3164, s32[]{:T(128)S(6)} %add.3165, s32[]{:T(128)S(6)} %add.3166, ...), kind=kLoop, calls=%fused_computation.490.clone.1 | loop fusion | flops 87949312 | bytes 119891768 | tf_op jit(solution)/shard_map/while/body/eval_jaxpr/add | solution.py:53
  647.2 72.7 %fusion.1134 = f32[16,1,44,512]{3,2,1,0:T(8,128)S(1)} fusion(f32[42,1,70,512]{3,2,1,0:T(8,128)} %get-tuple-element.2202, s32[]{:T(128)S(6)} %select_n.3518, s32[]{:T(128)S(6)} %add.3161, s32[]{:T(128)S(6)} %add.3162, s32[]{:T(128)S(6)} %add.3163, s32[]{:T(128)S(6)} %add.3164, s32[]{:T(128)S(6)} %add.3165, s32[]{:T(128)S(6)} %add.3166, ...), kind=kLoop, calls=%fused_computation.490.clone.1 | loop fusion | flops 87949312 | bytes 119891768 | tf_op jit(solution)/shard_map/while/body/eval_jaxpr/add | solution.py:53
  731.3 77.3 %fusion.1134 = f32[16,1,44,512]{3,2,1,0:T(8,128)S(1)} fusion(f32[42,1,70,512]{3,2,1,0:T(8,128)} %get-tuple-element.2202, s32[]{:T(128)S(6)} %select_n.3518, s32[]{:T(128)S(6)} %add.3161, s32[]{:T(128)S(6)} %add.3162, s32[]{:T(128)S(6)} %add.3163, s32[]{:T(128)S(6)} %add.3164, s32[]{:T(128)S(6)} %add.3165, s32[]{:T(128)S(6)} %add.3166, ...), kind=kLoop, calls=%fused_computation.490.clone.1 | loop fusion | flops 87949312 | bytes 119891768 | tf_op jit(solution)/shard_map/while/body/eval_jaxpr/add | solution.py:53
  819.7 72.8 %fusion.1134 = f32[16,1,44,512]{3,2,1,0:T(8,128)S(1)} fusion(f32[42,1,70,512]{3,2,1,0:T(8,128)} %get-tuple-element.2202, s32[]{:T(128)S(6)} %select_n.3518, s32[]{:T(128)S(6)} %add.3161, s32[]{:T(128)S(6)} %add.3162, s32[]{:T(128)S(6)} %add.3163, s32[]{:T(128)S(6)} %add.3164, s32[]{:T(128)S(6)} %add.3165, s32[]{:T(128)S(6)} %add.3166, ...), kind=kLoop, calls=%fused_computation.490.clone.1 | loop fusion | flops 87949312 | bytes 119891768 | tf_op jit(solution)/shard_map/while/body/eval_jaxpr/add | solution.py:53
  893.0 38.9 %all-reduce.8 = (f32[512]{0:T(512)S(1)}, f32[512]{0:T(512)S(1)}) all-reduce(f32[512]{0:T(512)S(1)} %get-tuple-element.525, f32[512]{0:T(512)S(1)} %get-tuple-element.524), channel_id=1, replica_groups=mesh['dp'=8,'rows'=4] {'dp','rows'}, use_global_device_ids=true, to_apply=%region_11.12 | all-reduce | flops 1024 | bytes 8192 | tf_op jit(solution)/shard_map/psum | solution.py:118
  939.1 40.1 %all-reduce.7 = (f32[512]{0:T(512)S(1)}, f32[512]{0:T(512)S(1)}) all-reduce(f32[512]{0:T(512)S(1)} %get-tuple-element.523, f32[512]{0:T(512)S(1)} %get-tuple-element.522), channel_id=1, replica_groups=mesh['dp'=8,'rows'=4] {'dp','rows'}, use_global_device_ids=true, to_apply=%region_15.16 | all-reduce | flops 1024 | bytes 8192 | tf_op jit(solution)/shard_map/psum | solution.py:118
  987.5 103.6 %all-gather.3.cloned.1.call-done = f32[64,1,44,512]{3,1,2,0:T(1,128)} async-done(((f32[16,1,44,512]{3,1,2,0:T(1,128)}), f32[64,1,44,512]{3,1,2,0:T(1,128)}) %all-gather.3.cloned.1.call-update) | async-done | bytes 5767184 | tf_op jit(solution)/shard_map/all_gather | solution.py:175
  1091.0 16.8 multiply_multiply_fusion.2
  1107.8 90.4 %all-gather.5.cloned.1.call-done = f32[64,1,44,512]{3,0,2,1:T(8,128)} async-done(((f32[16,1,44,512]{3,0,2,1:T(8,128)}), f32[64,1,44,512]{3,0,2,1:T(8,128)}) %all-gather.5.cloned.1.call-update) | async-done | bytes 5767184 | tf_op jit(solution)/shard_map/all_gather | solution.py:181
  1198.2 16.1 fusion.985
  1216.8 14.4 fusion.996
  1232.4 17.2 fusion.999
  1253.7 24.6 fusion.1053
  1278.3 25.5 fusion.1056
  1303.8 36.6 %reduce-scatter.5.cloned.1.call-done = f32[16,1,44,512]{3,2,0,1:T(8,128)} async-done(((f32[64,1,44,512]{3,2,0,1:T(8,128)}), f32[16,1,44,512]{3,2,0,1:T(8,128)}) %reduce-scatter.5.cloned.1.call-update) | async-done | bytes 1441808 | tf_op jit(solution)/shard_map/reduce_scatter | solution.py:185
  1342.6 44.2 %all-reduce.6 = (f32[512]{0:T(512)S(1)}, f32[512]{0:T(512)S(1)}) all-reduce(f32[512]{0:T(512)S(1)} %get-tuple-element.521, f32[512]{0:T(512)S(1)} %get-tuple-element.520), channel_id=1, replica_groups=mesh['dp'=8,'rows'=4] {'dp','rows'}, use_global_device_ids=true, to_apply=%region_21.22 | all-reduce | flops 1024 | bytes 8192 | tf_op jit(solution)/shard_map/psum | solution.py:135
  1387.5 67.4 %reduce-scatter.3.cloned.1.call-done = f32[16,1,44,512]{3,2,0,1:T(8,128)} async-done(((f32[64,1,44,512]{3,2,0,1:T(8,128)}), f32[16,1,44,512]{3,2,0,1:T(8,128)}) %reduce-scatter.3.cloned.1.call-update) | async-done | bytes 1441808 | tf_op jit(solution)/shard_map/reduce_scatter | solution.py:178
  1465.5 40.9 %all-reduce.5 = (f32[512]{0:T(512)S(1)}, f32[512]{0:T(512)S(1)}) all-reduce(f32[512]{0:T(512)S(1)} %get-tuple-element.527, f32[512]{0:T(512)S(1)} %get-tuple-element.526), channel_id=1, replica_groups=mesh['dp'=8,'rows'=4] {'dp','rows'}, use_global_device_ids=true, to_apply=%region_25.26 | all-reduce | flops 1024 | bytes 8192 | tf_op jit(solution)/shard_map/psum | solution.py:135
  1519.9 401.2 %while.38 = (s32[]{:T(128)}, f32[9,3,27,512]{3,2,1,0:T(8,128)}, s32[9]{0:T(128)S(1)}, s32[42,1,70]{2,0,1:T(8,128)S(1)}, s32[16,1,44]{2,0,1:T(8,128)S(1)}, /*inde...) while((s32[]{:T(128)}, f32[9,3,27,512]{3,2,1,0:T(8,128)}, ...), condition=%wide.region_115.116_spmd, body=%wide.region_33.115_spmd.sunk | while | flops 87687400 | bytes 152436944 | solution.py:89
  1525.6 8.7 fusion.1129
  1570.2 8.6 fusion.1129
  1614.7 9.1 fusion.1129
  1659.7 9.1 fusion.1129
  1704.7 8.2 fusion.1129
  1748.8 8.3 fusion.1129
  1793.0 8.8 fusion.1129
  1837.7 8.4 fusion.1129
  1882.0 8.6 fusion.1129
  1935.3 789.9 %while.40 = (s32[]{:T(128)}, f32[16,1,44,512]{3,2,1,0:T(8,128)}, s32[9]{0:T(128)S(1)}, s32[42,1,70]{2,0,1:T(8,128)S(1)}, s32[16,1,44]{2,0,1:T(8,128)S(1)}, /*ind...) while((s32[]{:T(128)}, f32[16,1,44,512]{3,2,1,0:T(8,128)}, ...), condition=%wide.region_27.28_spmd.clone, body=%wide.region_26.27_spmd.clone.sunk | while | flops 88006376 | bytes 132052736 | solution.py:61
  1946.8 75.3 %fusion.1138 = f32[16,1,44,512]{3,2,1,0:T(8,128)S(1)} fusion(f32[42,1,70,512]{3,2,1,0:T(8,128)} %get-tuple-element.2322, s32[]{:T(128)S(6)} %select_n.3603, s32[]{:T(128)S(6)} %add.3277, s32[]{:T(128)S(6)} %add.3278, s32[]{:T(128)S(6)} %add.3279, s32[]{:T(128)S(6)} %add.3280, s32[]{:T(128)S(6)} %add.3281, s32[]{:T(128)S(6)} %add.3282, ...), kind=kLoop, calls=%fused_computation.1057.clone.1 | loop fusion | flops 87949312 | bytes 119891768 | tf_op jit(solution)/shard_map/while/body/eval_jaxpr/add | solution.py:53
  2034.5 76.6 %fusion.1138 = f32[16,1,44,512]{3,2,1,0:T(8,128)S(1)} fusion(f32[42,1,70,512]{3,2,1,0:T(8,128)} %get-tuple-element.2322, s32[]{:T(128)S(6)} %select_n.3603, s32[]{:T(128)S(6)} %add.3277, s32[]{:T(128)S(6)} %add.3278, s32[]{:T(128)S(6)} %add.3279, s32[]{:T(128)S(6)} %add.3280, s32[]{:T(128)S(6)} %add.3281, s32[]{:T(128)S(6)} %add.3282, ...), kind=kLoop, calls=%fused_computation.1057.clone.1 | loop fusion | flops 87949312 | bytes 119891768 | tf_op jit(solution)/shard_map/while/body/eval_jaxpr/add | solution.py:53
  2123.5 76.2 %fusion.1138 = f32[16,1,44,512]{3,2,1,0:T(8,128)S(1)} fusion(f32[42,1,70,512]{3,2,1,0:T(8,128)} %get-tuple-element.2322, s32[]{:T(128)S(6)} %select_n.3603, s32[]{:T(128)S(6)} %add.3277, s32[]{:T(128)S(6)} %add.3278, s32[]{:T(128)S(6)} %add.3279, s32[]{:T(128)S(6)} %add.3280, s32[]{:T(128)S(6)} %add.3281, s32[]{:T(128)S(6)} %add.3282, ...), kind=kLoop, calls=%fused_computation.1057.clone.1 | loop fusion | flops 87949312 | bytes 119891768 | tf_op jit(solution)/shard_map/while/body/eval_jaxpr/add | solution.py:53
  2212.2 73.1 %fusion.1138 = f32[16,1,44,512]{3,2,1,0:T(8,128)S(1)} fusion(f32[42,1,70,512]{3,2,1,0:T(8,128)} %get-tuple-element.2322, s32[]{:T(128)S(6)} %select_n.3603, s32[]{:T(128)S(6)} %add.3277, s32[]{:T(128)S(6)} %add.3278, s32[]{:T(128)S(6)} %add.3279, s32[]{:T(128)S(6)} %add.3280, s32[]{:T(128)S(6)} %add.3281, s32[]{:T(128)S(6)} %add.3282, ...), kind=kLoop, calls=%fused_computation.1057.clone.1 | loop fusion | flops 87949312 | bytes 119891768 | tf_op jit(solution)/shard_map/while/body/eval_jaxpr/add | solution.py:53
  2297.6 74.7 %fusion.1138 = f32[16,1,44,512]{3,2,1,0:T(8,128)S(1)} fusion(f32[42,1,70,512]{3,2,1,0:T(8,128)} %get-tuple-element.2322, s32[]{:T(128)S(6)} %select_n.3603, s32[]{:T(128)S(6)} %add.3277, s32[]{:T(128)S(6)} %add.3278, s32[]{:T(128)S(6)} %add.3279, s32[]{:T(128)S(6)} %add.3280, s32[]{:T(128)S(6)} %add.3281, s32[]{:T(128)S(6)} %add.3282, ...), kind=kLoop, calls=%fused_computation.1057.clone.1 | loop fusion | flops 87949312 | bytes 119891768 | tf_op jit(solution)/shard_map/while/body/eval_jaxpr/add | solution.py:53
  2384.8 75.8 %fusion.1138 = f32[16,1,44,512]{3,2,1,0:T(8,128)S(1)} fusion(f32[42,1,70,512]{3,2,1,0:T(8,128)} %get-tuple-element.2322, s32[]{:T(128)S(6)} %select_n.3603, s32[]{:T(128)S(6)} %add.3277, s32[]{:T(128)S(6)} %add.3278, s32[]{:T(128)S(6)} %add.3279, s32[]{:T(128)S(6)} %add.3280, s32[]{:T(128)S(6)} %add.3281, s32[]{:T(128)S(6)} %add.3282, ...), kind=kLoop, calls=%fused_computation.1057.clone.1 | loop fusion | flops 87949312 | bytes 119891768 | tf_op jit(solution)/shard_map/while/body/eval_jaxpr/add | solution.py:53
  2473.1 74.4 %fusion.1138 = f32[16,1,44,512]{3,2,1,0:T(8,128)S(1)} fusion(f32[42,1,70,512]{3,2,1,0:T(8,128)} %get-tuple-element.2322, s32[]{:T(128)S(6)} %select_n.3603, s32[]{:T(128)S(6)} %add.3277, s32[]{:T(128)S(6)} %add.3278, s32[]{:T(128)S(6)} %add.3279, s32[]{:T(128)S(6)} %add.3280, s32[]{:T(128)S(6)} %add.3281, s32[]{:T(128)S(6)} %add.3282, ...), kind=kLoop, calls=%fused_computation.1057.clone.1 | loop fusion | flops 87949312 | bytes 119891768 | tf_op jit(solution)/shard_map/while/body/eval_jaxpr/add | solution.py:53
  2559.8 76.9 %fusion.1138 = f32[16,1,44,512]{3,2,1,0:T(8,128)S(1)} fusion(f32[42,1,70,512]{3,2,1,0:T(8,128)} %get-tuple-element.2322, s32[]{:T(128)S(6)} %select_n.3603, s32[]{:T(128)S(6)} %add.3277, s32[]{:T(128)S(6)} %add.3278, s32[]{:T(128)S(6)} %add.3279, s32[]{:T(128)S(6)} %add.3280, s32[]{:T(128)S(6)} %add.3281, s32[]{:T(128)S(6)} %add.3282, ...), kind=kLoop, calls=%fused_computation.1057.clone.1 | loop fusion | flops 87949312 | bytes 119891768 | tf_op jit(solution)/shard_map/while/body/eval_jaxpr/add | solution.py:53
  2649.2 74.8 %fusion.1138 = f32[16,1,44,512]{3,2,1,0:T(8,128)S(1)} fusion(f32[42,1,70,512]{3,2,1,0:T(8,128)} %get-tuple-element.2322, s32[]{:T(128)S(6)} %select_n.3603, s32[]{:T(128)S(6)} %add.3277, s32[]{:T(128)S(6)} %add.3278, s32[]{:T(128)S(6)} %add.3279, s32[]{:T(128)S(6)} %add.3280, s32[]{:T(128)S(6)} %add.3281, s32[]{:T(128)S(6)} %add.3282, ...), kind=kLoop, calls=%fused_computation.1057.clone.1 | loop fusion | flops 87949312 | bytes 119891768 | tf_op jit(solution)/shard_map/while/body/eval_jaxpr/add | solution.py:53
  2744.8 42.7 %all-reduce.4 = (f32[512]{0:T(512)S(1)}, f32[512]{0:T(512)S(1)}, f32[5,5,512]{2,1,0:T(8,128)}) all-reduce(f32[512]{0:T(512)S(1)} %get-tuple-element.1016, f32[512]{0:T(512)S(1)} %reduce_sum.1108, f32[5,5,512]{2,1,0:T(8,128)S(1)} %copy-done.24), channel_id=1, replica_groups=mesh['dp'=8,'rows'=4] {'dp','rows'}, use_global_device_ids=true, to_apply=%region_31.32 | all-reduce | flops 13824 | bytes 110592 | tf_op jit(solution)/shard_map/psum | solution.py:135
  2793.8 82.7 %all-reduce.15.cloned.1.call-done = (f32[512,512]{1,0:T(8,128)}, f32[27,27,512]{2,1,0:T(8,128)}, f32[512,512]{1,0:T(8,128)}) async-done(((f32[512,512]{1,0:T(8,128)}, f32[27,27,512]{2,1,0:T(8,128)}, f32[512,512]{1,0:T(8,128)}), (f32[512,512]{1,0:T(8,128)}, f32[27,27,512]{2,1,0:T(8,128)}, f32[512,512]{1,0:T(8,128)})) %all-reduce.15.cloned.1.call-update) | async-done | bytes 3590160 | tf_op jit(solution)/shard_map/psum | solution.py:223
  (541 shorter events, 530.1 us)
Async XLA Ops:
  7.2 1083.9 %copy-start = (f32[512,512]{1,0:T(8,128)S(1)}, f32[512,512]{1,0:T(8,128)}, u32[]{:S(2)}) copy-start(f32[512,512]{1,0:T(8,128)} %param.33) | copy-start | bytes 3145732
  7.2 46.9 %copy-start.7 = (f32[16,1,44,512]{3,1,2,0:T(1,128)S(1)}, f32[16,1,44,512]{3,1,2,0:T(1,128)}, u32[]{:S(2)}) copy-start(f32[16,1,44,512]{3,1,2,0:T(1,128)} %param.21) | copy-start | bytes 4325380
  7.2 1083.8 %all-gather.3.cloned.1.call-start = ((), (), s32[]{:S(2)}) async-start(), calls=%async_computation.2 | async-start | bytes 7208960 | tf_op jit(solution)/shard_map/all_gather | solution.py:175
  8.1 50.1 %copy-start.20 = (f32[16,1,44]{2,1,0:T(1,128)}, f32[16,1,44]{2,1,0:T(1,128)S(1)}, u32[]{:S(2)}) copy-start(f32[16,1,44]{2,1,0:T(1,128)S(1)} %compare_convert_fusion) | copy-start | bytes 8452
  62.5 14.1 copy-start.13
  62.5 14.1 copy-start.25
  62.5 35.8 %collective-permute-start.2 = (f32[13,1,44,512]{3,1,2,0:T(1,128)}, f32[13,1,44,512]{3,1,2,0:T(1,128)}, u32[]{:S(2)}, u32[]{:S(2)}) collective-permute-start(f32[13,1,44,512]{3,1,2,0:T(1,128)} %copy.85), channel_id=1, source_target_pairs={{0,1},{1,2},{2,3},{4,5},{5,6},{6,7},{8,9},{9,10},{10,11},{12,13},{... | collective-permute-start | bytes 3514376 | tf_op jit(solution)/shard_map/ppermute | solution.py:18
  69.3 30.5 %collective-permute-start.3 = (f32[13,1,44,512]{3,1,2,0:T(1,128)}, f32[13,1,44,512]{3,1,2,0:T(1,128)}, u32[]{:S(2)}, u32[]{:S(2)}) collective-permute-start(f32[13,1,44,512]{3,1,2,0:T(1,128)} %copy.86), channel_id=1, source_target_pairs={{1,0},{2,1},{3,2},{5,4},{6,5},{7,6},{9,8},{10,9},{11,10},{13,12},{... | collective-permute-start | bytes 3514376 | tf_op jit(solution)/shard_map/ppermute | solution.py:20
  70.6 20.3 collective-permute-start
  75.2 23.1 collective-permute-start.1
  104.6 788.0 %copy-start.21 = (f32[16,1,44]{2,1,0:T(1,128)S(1)}, f32[16,1,44]{2,1,0:T(1,128)}, u32[]{:S(2)}) copy-start(f32[16,1,44]{2,1,0:T(1,128)} %copy-done.20) | copy-start | bytes 8452
  892.6 567.7 %copy-start.2 = (f32[16,1,44,512]{3,2,1,0:T(8,128)}, f32[16,1,44,512]{3,2,1,0:T(8,128)S(1)}, u32[]{:S(2)}) copy-start(f32[16,1,44,512]{3,2,1,0:T(8,128)S(1)} %get-tuple-element.284) | copy-start | bytes 4325380
  892.6 40.0 %copy-start.37 = (f32[512]{0:T(512)S(1)}, f32[512]{0:T(512)}, u32[]{:S(2)}) copy-start(f32[512]{0:T(512)} %param.28) | copy-start | bytes 6148
  892.6 40.0 %copy-start.47 = (f32[512]{0:T(512)S(1)}, f32[512]{0:T(512)}, u32[]{:S(2)}) copy-start(f32[512]{0:T(512)} %param.29) | copy-start | bytes 6148
  932.5 574.5 %copy-start.31 = (f32[512]{0:T(512)}, f32[512]{0:T(512)S(1)}, u32[]{:S(2)}) copy-start(f32[512]{0:T(512)S(1)} %get-tuple-element.1008) | copy-start | bytes 6148
  932.5 574.5 %copy-start.33 = (f32[512]{0:T(512)}, f32[512]{0:T(512)S(1)}, u32[]{:S(2)}) copy-start(f32[512]{0:T(512)S(1)} %get-tuple-element.1009) | copy-start | bytes 6148
  932.6 47.3 %copy-start.35 = (f32[512]{0:T(512)S(1)}, f32[512]{0:T(512)}, u32[]{:S(2)}) copy-start(f32[512]{0:T(512)} %param.31) | copy-start | bytes 6148
  932.6 47.3 %copy-start.36 = (f32[512]{0:T(512)S(1)}, f32[512]{0:T(512)}, u32[]{:S(2)}) copy-start(f32[512]{0:T(512)} %param.32) | copy-start | bytes 6148
  984.2 214.0 %all-gather.5.cloned.1.call-start = ((), (), s32[]{:S(2)}) async-start(), calls=%async_computation.4 | async-start | bytes 7208960 | tf_op jit(solution)/shard_map/all_gather | solution.py:181
  987.4 352.9 %reduce-scatter.5.cloned.1.call-start = ((), (), s32[]{:S(2)}) async-start(), calls=%async_computation.5 | async-start | bytes 7864320 | tf_op jit(solution)/shard_map/reduce_scatter | solution.py:185
  1231.2 223.7 %reduce-scatter.3.cloned.1.call-start = ((), (), s32[]{:S(2)}) async-start(), calls=%async_computation.3 | async-start | bytes 7864320 | tf_op jit(solution)/shard_map/reduce_scatter | solution.py:178
  1249.6 1544.2 %all-reduce.17.cloned.1.call-start = ((), (), s32[]{:S(2)}) async-start(), calls=%async_computation.7 | async-start | bytes 4194304 | tf_op jit(solution)/shard_map/psum | solution.py:188
  1386.9 73.4 %copy-start.42 = (f32[512]{0:T(512)}, f32[512]{0:T(512)S(1)}, u32[]{:S(2)}) copy-start(f32[512]{0:T(512)S(1)} %get-tuple-element.2485) | copy-start | bytes 6148
  1386.9 73.4 %copy-start.45 = (f32[512]{0:T(512)}, f32[512]{0:T(512)S(1)}, u32[]{:S(2)}) copy-start(f32[512]{0:T(512)S(1)} %get-tuple-element.2484) | copy-start | bytes 6148
  1512.9 416.5 %collective-permute-start.4 = (f32[13,1,44,512]{3,1,2,0:T(1,128)}, f32[13,1,44,512]{3,1,2,0:T(1,128)}, u32[]{:S(2)}, u32[]{:S(2)}) collective-permute-start(f32[13,1,44,512]{3,1,2,0:T(1,128)} %copy.99), channel_id=1, source_target_pairs={{0,1},{1,2},{2,3},{4,5},{5,6},{6,7},{8,9},{9,10},{10,11},{12,13},{... | collective-permute-start | bytes 3514376 | tf_op jit(solution)/shard_map/ppermute | solution.py:18
  1518.6 412.3 %collective-permute-start.5 = (f32[13,1,44,512]{3,1,2,0:T(1,128)}, f32[13,1,44,512]{3,1,2,0:T(1,128)}, u32[]{:S(2)}, u32[]{:S(2)}) collective-permute-start(f32[13,1,44,512]{3,1,2,0:T(1,128)} %copy.100), channel_id=1, source_target_pairs={{1,0},{2,1},{3,2},{5,4},{6,5},{7,6},{9,8},{10,9},{11,10},{13,12},{... | collective-permute-start | bytes 3514376 | tf_op jit(solution)/shard_map/ppermute | solution.py:20
  1519.8 403.2 %copy-start.22 = (f32[16,1,44]{2,1,0:T(1,128)S(1)}, f32[16,1,44]{2,1,0:T(1,128)}, u32[]{:S(2)}) copy-start(f32[16,1,44]{2,1,0:T(1,128)} %copy-done.20) | copy-start | bytes 8452
  1519.9 403.2 %copy-start.32 = (f32[512]{0:T(512)S(1)}, f32[512]{0:T(512)}, u32[]{:S(2)}) copy-start(f32[512]{0:T(512)} %copy-done.31) | copy-start | bytes 6148
  1519.9 403.2 %copy-start.34 = (f32[512]{0:T(512)S(1)}, f32[512]{0:T(512)}, u32[]{:S(2)}) copy-start(f32[512]{0:T(512)} %copy-done.33) | copy-start | bytes 6148
  1519.9 403.2 %copy-start.38 = (f32[512]{0:T(512)S(1)}, f32[512]{0:T(512)}, u32[]{:S(2)}) copy-start(f32[512]{0:T(512)} %param.28) | copy-start | bytes 6148
  1519.9 403.2 %copy-start.48 = (f32[512]{0:T(512)S(1)}, f32[512]{0:T(512)}, u32[]{:S(2)}) copy-start(f32[512]{0:T(512)} %param.29) | copy-start | bytes 6148
  1659.7 9.1 slice-start
  1659.7 9.1 slice-start.1
  1922.6 953.9 %all-reduce.15.cloned.1.call-start = ((), (), s32[]{:S(2)}) async-start(), calls=%async_computation.6 | async-start | bytes 7733248 | tf_op jit(solution)/shard_map/psum | solution.py:223
  1935.3 789.9 %copy-start.23 = (f32[16,1,44]{2,1,0:T(1,128)S(1)}, f32[16,1,44]{2,1,0:T(1,128)}, u32[]{:S(2)}) copy-start(f32[16,1,44]{2,1,0:T(1,128)} %copy-done.20) | copy-start | bytes 8452
  1935.3 790.0 %copy-start.27 = (f32[512]{0:T(512)S(1)}, f32[512]{0:T(512)}, u32[]{:S(2)}) copy-start(f32[512]{0:T(512)} %copy-done.26) | copy-start | bytes 6148
  1935.3 790.0 %copy-start.29 = (f32[512]{0:T(512)S(1)}, f32[512]{0:T(512)}, u32[]{:S(2)}) copy-start(f32[512]{0:T(512)} %copy-done.28) | copy-start | bytes 6148
  1935.3 790.0 %copy-start.30 = (f32[512]{0:T(512)S(1)}, f32[512]{0:T(512)}, u32[]{:S(2)}) copy-start(f32[512]{0:T(512)} %param.23) | copy-start | bytes 6148
  1935.3 790.0 %copy-start.39 = (f32[512]{0:T(512)S(1)}, f32[512]{0:T(512)}, u32[]{:S(2)}) copy-start(f32[512]{0:T(512)} %param.24) | copy-start | bytes 6148
  1935.3 11.5 copy-start.3
  2023.3 11.2 copy-start.3
  2112.3 11.3 copy-start.3
  2200.9 11.3 copy-start.3
  2286.4 11.2 copy-start.3
  2373.5 11.4 copy-start.3
  2461.8 11.3 copy-start.3
  2548.7 11.1 copy-start.3
  2637.8 11.4 copy-start.3
  (47 other events, 222.0 us)
Sparse Core Ops, SparseCore 0:
  984.3 106.6 all-gather.2
  1093.2 104.9 all-gather.4
  1231.3 108.9 reduce-scatter.4
  1342.5 112.3 reduce-scatter.2
  1459.2 62.4 all-reduce.16
  2732.8 143.6 all-reduce.14
where the time goes:
time: 2910 us; the launch traced here: 2890 us
  other arithmetic  1760 us (60%)
  waiting for transfers between devices  401 us (14%)
  blocking collectives  249 us (9%)
  local copies, waits for them, and re-layouts  152 us (5%)
  matrix products  151 us (5%)
  loops' own time  147 us (5%)
    add x18, other arithmetic, depthwise_row_step(): running + jnp.where(same_image, row_slab[:, :, column:column + width_coun...  1360 us
    reduce_sum x99, other arithmetic, kernel_row_step(): jnp.sum(jnp.where(same_image, row_slab[:, :, column:column + width_count]...  340 us
    psum x3, blocking collectives, denormalize(): lax.psum((jnp.sum(masked, axis=(0, 1, 2)), jnp.sum(masked * normed, axis=...  128 us
    psum x3, blocking collectives, apply_layer_norm(): lax.psum((jnp.sum(valid_field, axis=(0, 1, 2)), jnp.sum(valid_field * fie...  121 us
    another operation x2, loops' own time, depthwise(): result, ignored_value = lax.scan(depthwise_row_step, start_sum, offsets)  106 us
    all_gather x1, waiting for transfers between devices, shards(): gathered = lax.all_gather(third_normed_output, 'rows', axis=0, tiled=True)  104 us
    all_gather x1, waiting for transfers between devices, shards(): grad_gathered = lax.all_gather(out_grad, 'rows', axis=0, tiled=True)  90.4 us
    dot_general x8, matrix products, product(): jnp.dot(left, right, precision=HIGHEST, preferred_element_type=jnp.float32)  86.7 us
  transfers between devices with their start and end apart: 12, of which 7 were waited for; matrix products, arithmetic and copies ran while one was open for 43% of the time, Pallas kernels for 0%

commit v1 on v0

v1 whole, which is shorter than its diff:
```python
import functools

import jax
import jax.numpy as jnp
import numpy as np
from jax import lax
from jax.experimental import pallas as pl
from jax.experimental.pallas import tpu as pltpu
from jax.sharding import PartitionSpec as P

EPSILON = 1e-05
HIGHEST = lax.Precision.HIGHEST
HIGH = lax.Precision.HIGH
MESH = pl.DeviceIdType.MESH
F32 = jnp.float32
BF16 = jnp.bfloat16

LEFT, RIGHT = 24, 16
SLOTS = LEFT + RIGHT
LEFT_IDS = 3
LEFT_N, RIGHT_N = 37, 27
LEFT_F, RIGHT_F = 24, 16
FREQ = 2 * LEFT_F + 2 * RIGHT_F
REACH = 13
SPAN = 2 * REACH + 1
SPAN_PAD = 32


def forward_transform(length, padded, positions, columns):
    count = length // 2 + 1
    out = np.zeros((2 * padded, columns))
    angle = 2 * np.pi * np.outer(np.arange(count), positions) / length
    out[:count, : len(positions)] = np.cos(angle)
    out[padded : padded + count, : len(positions)] = -np.sin(angle)
    return out


def backward_transform(length, padded, positions, rows):
    count = length // 2 + 1
    out = np.zeros((rows, 2 * padded))
    twice = np.where(np.arange(count) == 0, 1.0, 2.0)
    angle = 2 * np.pi * np.outer(positions, np.arange(count)) / length
    out[: len(positions), :count] = np.cos(angle) * twice / length
    out[: len(positions), padded : padded + count] = -np.sin(angle) * twice / length
    return out


def slots_to_freq():
    out = np.zeros((FREQ, SLOTS))
    out[: 2 * LEFT_F, :LEFT] = forward_transform(LEFT_N, LEFT_F, np.arange(LEFT), LEFT)
    out[2 * LEFT_F :, LEFT:] = forward_transform(RIGHT_N, RIGHT_F, np.arange(RIGHT), RIGHT)
    return out


def freq_to_slots():
    out = np.zeros((SLOTS, FREQ))
    out[:LEFT, : 2 * LEFT_F] = backward_transform(LEFT_N, LEFT_F, np.arange(LEFT), LEFT)
    out[LEFT:, 2 * LEFT_F :] = backward_transform(RIGHT_N, RIGHT_F, np.arange(RIGHT), RIGHT)
    return out


def taps_to_freq():
    taps = np.arange(SPAN) - REACH
    return np.concatenate(
        [
            forward_transform(LEFT_N, LEFT_F, taps, SPAN_PAD),
            forward_transform(RIGHT_N, RIGHT_F, taps, SPAN_PAD),
        ]
    )


def freq_to_taps():
    taps = np.arange(SPAN) - REACH
    return np.concatenate(
        [
            backward_transform(LEFT_N, LEFT_F, taps, SPAN_PAD),
            backward_transform(RIGHT_N, RIGHT_F, taps, SPAN_PAD),
        ],
        axis=1,
    )


def split_constant(matrix, group):
    whole = np.kron(np.eye(group), matrix).astype(np.float32)
    high = whole.astype(jnp.bfloat16)
    low = (whole - high.astype(np.float32)).astype(jnp.bfloat16)
    return np.concatenate([high, high, low], axis=1)


def split_stack(value):
    high = value.astype(BF16)
    low = (value - high.astype(F32)).astype(BF16)
    return jnp.concatenate([high, low, high], axis=0)


def product_split(constant_ref, value):
    return jnp.dot(constant_ref[...], split_stack(value), preferred_element_type=F32)


GROUP_IN = 6
GROUP_OUT = 4
GROUP_TAP = 7
GROUP_GRAD = 4


def transform_window(rows, window, to_freq_ref, out_ref):
    for first in range(0, rows, GROUP_IN):
        part = window[first * SLOTS : (first + GROUP_IN) * SLOTS, :]
        freq = product_split(to_freq_ref, part)
        out_ref[first : first + GROUP_IN] = freq.reshape(GROUP_IN, FREQ, freq.shape[-1])


def fill_window(window, top_ref, own_ref, bottom_ref):
    at = 0
    for ref in (top_ref, own_ref, bottom_ref):
        rows = ref.shape[0]
        window[at : at + rows * SLOTS, :] = ref[...].reshape(rows * SLOTS, ref.shape[-1])
        at += rows * SLOTS


def sum_rows(bounds, rows, x_ref, k_ref, y_ref, flipped, conjugate):
    width = x_ref.shape[-1]
    for side, (start, size) in enumerate(((0, LEFT_F), (2 * LEFT_F, RIGHT_F))):
        real, imag = pl.ds(start, size), pl.ds(start + size, size)

        def one_row(row, carry):
            def tap(w, total):
                index = row + SPAN - 1 - w if flipped else w - row
                xr, xi = x_ref[w, real, :], x_ref[w, imag, :]
                kr, ki = k_ref[index, real, :], k_ref[index, imag, :]
                if conjugate:
                    return (total[0] + kr * xr + ki * xi, total[1] + kr * xi - ki * xr)
                return (total[0] + kr * xr - ki * xi, total[1] + kr * xi + ki * xr)

            zero = jnp.zeros((size, width), F32)
            low, high = bounds[2 * side, row], bounds[2 * side + 1, row]
            yr, yi = lax.fori_loop(low, high, tap, (zero, zero))
            y_ref[row, real, :] = yr
            y_ref[row, imag, :] = yi
            return carry

        lax.fori_loop(0, rows, one_row, 0)


def rows_to_slots(rows, y_ref, to_slots_ref, mask_ref, out_ref):
    for first in range(0, rows, GROUP_OUT):
        freq = y_ref[first : first + GROUP_OUT].reshape(GROUP_OUT * FREQ, y_ref.shape[-1])
        cells = product_split(to_slots_ref, freq).reshape(GROUP_OUT, SLOTS, y_ref.shape[-1])
        out_ref[first : first + GROUP_OUT] = cells * mask_ref[first : first + GROUP_OUT]


def conv_forward_kernel(
    bounds, top, own, bottom, taps, mask, to_freq, taps_freq, to_slots, out, xf, kf, stats, window, yf
):
    rows = own.shape[0]
    fill_window(window, top, own, bottom)
    transform_window(rows + 2 * REACH, window, to_freq, xf)
    for first in range(0, kf.shape[0], GROUP_TAP):
        part = taps[first : first + GROUP_TAP].reshape(GROUP_TAP * SPAN_PAD, taps.shape[-1])
        freq = product_split(taps_freq, part)
        kf[first : first + GROUP_TAP] = freq.reshape(GROUP_TAP, FREQ, freq.shape[-1])
    sum_rows(bounds, rows, xf, kf, yf, False, True)
    rows_to_slots(rows, yf, to_slots, mask, out)
    cells = out[...].reshape(rows * SLOTS, out.shape[-1])
    stats[0:1, :] = jnp.sum(cells, axis=0, keepdims=True)
    stats[1:2, :] = jnp.sum(cells * cells, axis=0, keepdims=True)
    stats[2:8, :] = jnp.zeros((6, stats.shape[-1]), F32)


def conv_backward_kernel(
    bounds, top, own, bottom, xf, kf, mask, to_freq, to_slots, to_taps, out, grad, window, df, yf, gf
):
    rows = own.shape[0]
    width = own.shape[-1]
    fill_window(window, top, own, bottom)
    transform_window(rows + 2 * REACH, window, to_freq, df)
    sum_rows(bounds, rows, df, kf, yf, True, False)
    rows_to_slots(rows, yf, to_slots, mask, out)
    gf[...] = jnp.zeros(gf.shape, F32)
    for side, (start, size) in enumerate(((0, LEFT_F), (2 * LEFT_F, RIGHT_F))):
        real, imag = pl.ds(start, size), pl.ds(start + size, size)

        def one_row(row, carry):
            dr, di = df[row + REACH, real, :], df[row + REACH, imag, :]

            def tap(w, inner):
                xr, xi = xf[w, real, :], xf[w, imag, :]
                gf[w - row, real, :] += dr * xr + di * xi
                gf[w - row, imag, :] += dr * xi - di * xr
                return inner

            lax.fori_loop(bounds[2 * side, row], bounds[2 * side + 1, row], tap, 0)
            return carry

        lax.fori_loop(0, rows, one_row, 0)
    for first in range(0, gf.shape[0], GROUP_GRAD):
        freq = gf[first : first + GROUP_GRAD].reshape(GROUP_GRAD * FREQ, width)
        cells = product_split(to_taps, freq).reshape(GROUP_GRAD, SPAN_PAD, width)
        grad[first : first + GROUP_GRAD] = cells


CHUNK = 256
TAP_ROWS = 28


def chunked(leading):
    return pl.BlockSpec(leading + (CHUNK,), lambda c, *_: (0,) * len(leading) + (c,))


def whole(array):
    return pl.BlockSpec(array.shape, lambda c, *_: (0,) * array.ndim)


def conv_forward(bounds, top, own, bottom, taps, mask):
    rows, _, channels = own.shape
    window = rows + 2 * REACH
    constants = [
        jnp.asarray(split_constant(slots_to_freq(), GROUP_IN)),
        jnp.asarray(split_constant(taps_to_freq(), GROUP_TAP)),
        jnp.asarray(split_constant(freq_to_slots(), GROUP_OUT)),
    ]
    return pl.pallas_call(
        conv_forward_kernel,
        grid_spec=pltpu.PrefetchScalarGridSpec(
            num_scalar_prefetch=1,
            grid=(channels // CHUNK,),
            in_specs=[
                chunked((REACH, SLOTS)),
                chunked((rows, SLOTS)),
                chunked((REACH, SLOTS)),
                chunked((TAP_ROWS, SPAN_PAD)),
                pl.BlockSpec((rows, SLOTS, CHUNK), lambda c, *_: (0, 0, 0)),
            ]
            + [whole(c) for c in constants],
            out_specs=[
                chunked((rows, SLOTS)),
                chunked((window, FREQ)),
                chunked((TAP_ROWS, FREQ)),
                chunked((8,)),
            ],
            scratch_shapes=[
                pltpu.VMEM((window * SLOTS, CHUNK), F32),
                pltpu.VMEM((rows, FREQ, CHUNK), F32),
            ],
        ),
        out_shape=[
            jax.ShapeDtypeStruct((rows, SLOTS, channels), F32),
            jax.ShapeDtypeStruct((window, FREQ, channels), F32),
            jax.ShapeDtypeStruct((TAP_ROWS, FREQ, channels), F32),
            jax.ShapeDtypeStruct((8, channels), F32),
        ],
        compiler_params=pltpu.CompilerParams(vmem_limit_bytes=56 << 20),
        name="conv_forward",
    )(bounds, top, own, bottom, taps, mask, *constants)


def conv_backward(bounds, top, own, bottom, xf, kf, mask):
    rows, _, channels = own.shape
    window = rows + 2 * REACH
    constants = [
        jnp.asarray(split_constant(slots_to_freq(), GROUP_IN)),
        jnp.asarray(split_constant(freq_to_slots(), GROUP_OUT)),
        jnp.asarray(split_constant(freq_to_taps(), GROUP_GRAD)),
    ]
    return pl.pallas_call(
        conv_backward_kernel,
        grid_spec=pltpu.PrefetchScalarGridSpec(
            num_scalar_prefetch=1,
            grid=(channels // CHUNK,),
            in_specs=[
                chunked((REACH, SLOTS)),
                chunked((rows, SLOTS)),
                chunked((REACH, SLOTS)),
                chunked((window, FREQ)),
                chunked((TAP_ROWS, FREQ)),
                pl.BlockSpec((rows, SLOTS, CHUNK), lambda c, *_: (0, 0, 0)),
            ]
            + [whole(c) for c in constants],
            out_specs=[chunked((rows, SLOTS)), chunked((TAP_ROWS, SPAN_PAD))],
            scratch_shapes=[
                pltpu.VMEM((window * SLOTS, CHUNK), F32),
                pltpu.VMEM((window, FREQ, CHUNK), F32),
                pltpu.VMEM((rows, FREQ, CHUNK), F32),
                pltpu.VMEM((TAP_ROWS, FREQ, CHUNK), F32),
            ],
        ),
        out_shape=[
            jax.ShapeDtypeStruct((rows, SLOTS, channels), F32),
            jax.ShapeDtypeStruct((TAP_ROWS, SPAN_PAD, channels), F32),
        ],
        compiler_params=pltpu.CompilerParams(vmem_limit_bytes=56 << 20),
        name="conv_backward",
    )(bounds, top, own, bottom, xf, kf, mask, *constants)


def all_sum_kernel(dp, rows, x_ref, out_ref, slots, own_sem, send_sem, recv_sem):
    count = dp * rows
    me = lax.axis_index("dp") * rows + lax.axis_index("rows")
    barrier = pltpu.get_barrier_semaphore()

    def place(step):
        other = lax.rem(me + step, count)
        return (other // rows, lax.rem(other, rows))

    def greet(step, carry):
        pl.semaphore_signal(barrier, inc=1, device_id=place(step), device_id_type=MESH)
        return carry

    lax.fori_loop(1, count, greet, 0)
    own = pltpu.make_async_copy(x_ref, slots.at[me], own_sem)
    own.start()
    pl.semaphore_wait(barrier, count - 1)

    def send(step, carry):
        pltpu.make_async_remote_copy(
            src_ref=x_ref,
            dst_ref=slots.at[me],
            send_sem=send_sem,
            recv_sem=recv_sem,
            device_id=place(step),
            device_id_type=MESH,
        ).start()
        return carry

    lax.fori_loop(1, count, send, 0)
    own.wait()
    others = slots.at[pl.ds(0, count - 1)]
    pltpu.make_async_copy(others, others, recv_sem).wait()
    pltpu.make_async_copy(others, others, send_sem).wait()
    total = slots[0]
    for index in range(1, count):
        total = total + slots[index]
    out_ref[...] = total


def all_sum(value, dp, rows, collective_id):
    return pl.pallas_call(
        functools.partial(all_sum_kernel, dp, rows),
        out_shape=jax.ShapeDtypeStruct(value.shape, F32),
        in_specs=[pl.BlockSpec(memory_space=pltpu.VMEM)],
        out_specs=pl.BlockSpec(memory_space=pltpu.VMEM),
        scratch_shapes=[
            pltpu.VMEM((dp * rows,) + value.shape, F32),
            pltpu.SemaphoreType.DMA,
            pltpu.SemaphoreType.DMA,
            pltpu.SemaphoreType.DMA,
        ],
        compiler_params=pltpu.CompilerParams(
            collective_id=collective_id, has_side_effects=True, vmem_limit_bytes=32 << 20
        ),
        name="all_sum",
    )(value)


def neighbours(cells, width):
    count = lax.axis_size("rows")
    down = [(i, i + 1) for i in range(count - 1)]
    up = [(i + 1, i) for i in range(count - 1)]
    return (
        lax.ppermute(cells[-width:], "rows", down),
        lax.ppermute(cells[:width], "rows", up),
    )


def gelu_parts(x):
    scale, cubic = 0.7978845608028654, 0.044715
    square = x * x
    t = jnp.tanh(scale * (x + cubic * (x * square)))
    half = 0.5 * (1.0 + t)
    return (x * half, half + 0.5 * x * (1.0 - t * t) * (scale * (1.0 + 3.0 * cubic * square)))


def product(left, right):
    return jnp.dot(left, right, precision=HIGH, preferred_element_type=F32)


def product_t(left, right):
    return lax.dot_general(left, right, (((1,), (1,)), ((), ())), precision=HIGH, preferred_element_type=F32)


def contract(left, right):
    return lax.dot_general(left, right, (((0,), (0,)), ((), ())), precision=HIGH, preferred_element_type=F32)


def shards(
    dp,
    devices_rows,
    inputs,
    image_ids,
    first_norm_gain,
    first_norm_bias,
    point_one,
    kernel_big,
    kernel_small,
    second_norm_gain,
    second_norm_bias,
    point_two,
    feedforward_norm_gain,
    feedforward_norm_bias,
    w_up,
    w_down,
    out_grad,
):
    rows, canvases, columns, channels = inputs.shape
    assert canvases == 1 and kernel_big.shape[0] == SPAN
    pixels = rows * SLOTS
    ids = image_ids[:, 0]
    w_up_all = lax.all_gather(w_up, "rows")
    w_down_all = lax.all_gather(w_down, "rows")

    place = jnp.arange(columns, dtype=jnp.int32)[None, :]
    is_left = (ids >= 0) & (ids < LEFT_IDS)
    is_right = ids >= LEFT_IDS

    def side(member, width):
        name = jnp.max(jnp.where(member, ids, -1), axis=1)
        first = jnp.min(jnp.where(member, place, columns), axis=1)
        return name, jnp.minimum(first, columns - width)

    left_id, left_at = side(is_left, LEFT)
    right_id, right_at = side(is_right, RIGHT)
    slot_column = jnp.concatenate(
        [
            left_at[:, None] + jnp.arange(LEFT, dtype=jnp.int32)[None, :],
            right_at[:, None] + jnp.arange(RIGHT, dtype=jnp.int32)[None, :],
        ],
        axis=1,
    )
    slot_id = jnp.concatenate(
        [
            jnp.broadcast_to(left_id[:, None], (rows, LEFT)),
            jnp.broadcast_to(right_id[:, None], (rows, RIGHT)),
        ],
        axis=1,
    )
    hit = (slot_column[:, :, None] == place[:, None, :]) & (ids[:, None, :] == slot_id[:, :, None])
    hit = hit & (slot_id[:, :, None] >= 0)
    pick = hit.astype(F32)
    slot_mask = jnp.max(pick, axis=2)
    valid = (ids >= 0).astype(F32)

    names = jnp.stack([left_id, right_id], axis=1) + 1
    above, below = neighbours(names, REACH)
    window_names = jnp.concatenate([above, names, below], axis=0)
    window_rows = rows + 2 * REACH
    w_index = jnp.arange(window_rows, dtype=jnp.int32)[None, :]
    r_index = jnp.arange(rows, dtype=jnp.int32)[:, None]
    near = (w_index >= r_index) & (w_index <= r_index + 2 * REACH)
    bounds = []
    for which in range(2):
        same = near & (names[:, which][:, None] == window_names[:, which][None, :]) & (names[:, which][:, None] > 0)
        low = jnp.min(jnp.where(same, w_index, window_rows), axis=1)
        high = jnp.max(jnp.where(same, w_index + 1, 0), axis=1)
        bounds += [jnp.minimum(low, high), high]
    bounds = jnp.stack(bounds).astype(jnp.int32)

    def compact(field):
        out = lax.dot_general(
            pick, field[:, 0], (((2,), (1,)), ((0,), (0,))), precision=HIGHEST, preferred_element_type=F32
        )
        return out.reshape(pixels, channels)

    def expand(cells):
        return lax.dot_general(
            pick,
            cells.reshape(rows, SLOTS, channels),
            (((1,), (1,)), ((0,), (0,))),
            precision=HIGHEST,
            preferred_element_type=F32,
        )[:, None]

    mask = slot_mask.reshape(pixels, 1)
    mask_wide = jnp.broadcast_to(slot_mask[:, :, None], (rows, SLOTS, CHUNK))

    def stack_rows(*rows_list):
        pad = jnp.zeros((8 - len(rows_list), channels), F32)
        return jnp.concatenate([row.reshape(1, channels) for row in rows_list] + [pad], axis=0)

    x = compact(inputs)
    gy = compact(out_grad)

    def sums(field):
        return jnp.sum(field, axis=0), jnp.sum(field * field, axis=0)

    total = all_sum(
        stack_rows(*sums(x), jnp.full((channels,), jnp.sum(valid))), dp, devices_rows, 0
    )
    count = total[2, 0]

    def norm_scale(total):
        mean = total[0] / count
        return mean, lax.rsqrt(total[1] / count - mean * mean + EPSILON)

    mean_one, inv_one = norm_scale(total)
    xhat_one = (x - mean_one) * inv_one
    u1 = (xhat_one * first_norm_gain + first_norm_bias) * mask
    h1 = product(u1, point_one)
    act, act_slope = gelu_parts(h1)
    act = act.reshape(rows, SLOTS, channels)
    small_start = REACH - kernel_small.shape[0] // 2
    edge = (small_start, small_start)
    kernel = kernel_big + jnp.pad(kernel_small, (edge, edge, (0, 0)))
    taps = jnp.pad(kernel, ((0, TAP_ROWS - SPAN), (0, SPAN_PAD - SPAN), (0, 0)))
    act_above, act_below = neighbours(act, REACH)
    conv, xf, kf, conv_sums = conv_forward(bounds, act_above, act, act_below, taps, mask_wide)
    conv = conv.reshape(pixels, channels)
    mean_two, inv_two = norm_scale(all_sum(conv_sums, dp, devices_rows, 1))
    xhat_two = (conv - mean_two) * inv_two
    u2 = (xhat_two * second_norm_gain + second_norm_bias) * mask
    act2, act2_slope = gelu_parts(u2)
    mixed = x + product(act2, point_two)
    mixed_masked = mixed * mask
    mean_three, inv_three = norm_scale(
        all_sum(stack_rows(*sums(mixed_masked)), dp, devices_rows, 2)
    )
    xhat_three = (mixed - mean_three) * inv_three
    u3 = (xhat_three * feedforward_norm_gain + feedforward_norm_bias) * mask

    ffn = jnp.zeros((pixels, channels), F32)
    du3 = jnp.zeros((pixels, channels), F32)
    grad_up, grad_down = [], []
    for part in range(devices_rows):
        up, down = w_up_all[part], w_down_all[part]
        hid, slope = gelu_parts(product(u3, up))
        ffn = ffn + product(hid, down)
        dpre = product_t(gy, down) * slope
        du3 = du3 + product_t(dpre, up)
        grad_up.append(contract(u3, dpre))
        grad_down.append(contract(hid, gy))
    grad_w = lax.psum_scatter(
        jnp.stack([jnp.stack(grad_up), jnp.stack(grad_down)], axis=1), "rows", scatter_dimension=0, tiled=False
    )
    grad_w = lax.psum(grad_w, "dp")

    def norm_back(dy, xhat, inv, gain, number):
        masked = dy * mask
        total = all_sum(
            stack_rows(jnp.sum(masked, axis=0), jnp.sum(masked * xhat, axis=0)), dp, devices_rows, number
        )
        grad_bias, grad_gain = total[0], total[1]
        field = mask * gain * inv * (masked - grad_bias / count - xhat * (grad_gain / count))
        return field, grad_gain, grad_bias

    back_three, grad_gain_three, grad_bias_three = norm_back(
        du3, xhat_three, inv_three, feedforward_norm_gain, 3
    )
    dmixed = gy + back_three
    grad_point_two = contract(act2, dmixed)
    du2 = product_t(dmixed, point_two) * act2_slope
    dconv, grad_gain_two, grad_bias_two = norm_back(du2, xhat_two, inv_two, second_norm_gain, 4)
    dconv = dconv.reshape(rows, SLOTS, channels)
    d_above, d_below = neighbours(dconv, REACH)
    dact, grad_taps = conv_backward(bounds, d_above, dconv, d_below, xf, kf, mask_wide)
    dh1 = dact.reshape(pixels, channels) * act_slope
    grad_point_one = contract(u1, dh1)
    du1 = product_t(dh1, point_one)
    back_one, grad_gain_one, grad_bias_one = norm_back(du1, xhat_one, inv_one, first_norm_gain, 5)
    grad_cells = back_three + back_one
    output = inputs + expand((mixed - x) + ffn)
    grad_input = out_grad + expand(grad_cells)
    grad_point_one, grad_point_two, grad_kernel = lax.psum(
        (grad_point_one, grad_point_two, grad_taps[:SPAN, :SPAN]), ("dp", "rows")
    )
    small_end = small_start + kernel_small.shape[0]
    grad_small = grad_kernel[small_start:small_end, small_start:small_end]
    return (
        output,
        grad_input,
        grad_gain_one,
        grad_bias_one,
        grad_point_one,
        grad_kernel,
        grad_small,
        grad_gain_two,
        grad_bias_two,
        grad_point_two,
        grad_gain_three,
        grad_bias_three,
        grad_w[0],
        grad_w[1],
    )


def solution(mesh):
    field = P("rows", "dp", None, None)
    everywhere = P()
    up, down = P(None, "rows"), P("rows", None)
    return jax.shard_map(
        functools.partial(shards, mesh.shape["dp"], mesh.shape["rows"]),
        mesh=mesh,
        in_specs=(field, P("rows", "dp", None)) + (everywhere,) * 10 + (up, down, field),
        out_specs=(field, field) + (everywhere,) * 10 + (up, down),
        check_vma=False,
    )
```

time: 2910 us -> 833 us (0.29)
  other arithmetic: 1760 us -> 21.3 us
  blocking collectives: 249 us -> 0 us
  Pallas kernels: 0 us -> 236 us
  loops' own time: 147 us -> 0 us
  local copies, waits for them, and re-layouts: 152 us -> 38.1 us
  matrix products: 151 us -> 75.8 us
    add x21 -> x7, other arithmetic: 1370 us -> 2.65 us  [the longest x1 2.26 us: shards(): grad_cells = back_three + back_one]
    reduce_sum x104 -> x1, other arithmetic: 347 us -> 0.61 us  [shards(): jnp.sum(valid)]
    psum x6 -> x0, blocking collectives: 249 us -> none  [the longest x3 128 us: denormalize(): lax.psum((jnp.sum(masked, axis=(0, 1, 2)), jnp.sum(masked * normed, axis=...]
    pallas_call x0 -> x8, Pallas kernels: none -> 236 us  [the longest x6 177 us: all_sum(): pl.pallas_call(functools.partial(all_sum_kernel, dp, rows), out_shape=jax...]
    all_gather x2, waiting for transfers between devices: 194 us -> 0.02 us  [the longest x1 0.02 us: shards(): w_up_all = lax.all_gather(w_up, 'rows')]
    another operation x3 -> x0, loops' own time: 147 us -> none  [the longest x2 106 us: depthwise(): result, ignored_value = lax.scan(depthwise_row_step, start_sum, offsets)]
    unnamed x6, waiting for transfers between devices: 0.1 us -> 119 us
    reduce_scatter x2 -> x0, waiting for transfers between devices: 104 us -> none  [the longest x1 67.4 us: shards(): lax.psum_scatter(product(hidden_act, w_down), 'rows', scatter_dimension=0...]
  transfers between devices with their start and end apart: 12 -> 11, of which waited for: 7 -> 7; matrix products, arithmetic and copies ran while one was open for 43% -> 12% of each run, Pallas kernels for 0% -> 29%
where the time goes in v1:
time: 833 us; the launch traced here: 825 us
  waiting for transfers between devices  418 us (50%)
  Pallas kernels  236 us (28%)
  matrix products  75.8 us (9%)
  local copies, waits for them, and re-layouts  38.1 us (5%)
  other arithmetic  21.3 us (3%)
  starting transfers between devices  20.2 us (2%)
  between operations  15.3 us (2%)
    pallas_call x6, Pallas kernels, all_sum(): pl.pallas_call(functools.partial(all_sum_kernel, dp, rows), out_shape=jax...  177 us
    psum x1, waiting for transfers between devices, shards(): lax.psum((grad_point_one, grad_point_two, grad_taps[:SPAN, :SPAN]), ('dp'...  119 us
    unnamed x6, waiting for transfers between devices  119 us
    ppermute x3, waiting for transfers between devices, neighbours(): lax.ppermute(cells[-width:], 'rows', down)  77.2 us
    psum x1, waiting for transfers between devices, shards(): grad_w = lax.psum(grad_w, 'dp')  62.6 us
    ppermute x3, waiting for transfers between devices, neighbours(): lax.ppermute(cells[:width], 'rows', up)  40.7 us
    pallas_call x1, Pallas kernels, conv_backward(): pl.pallas_call(conv_backward_kernel, grid_spec=pltpu.PrefetchScalarGridSp...  35.2 us
    dot_general x10, matrix products, product(): return jnp.dot(left, right, precision=HIGH, preferred_element_type=F32)  23.8 us
  transfers between devices with their start and end apart: 11, of which 7 were waited for; matrix products, arithmetic and copies ran while one was open for 12% of the time, Pallas kernels for 29%

profile of v1, /device:TPU:0, one launch (start us, length us, event | category | flops | bytes accessed | tf_op | source)
XLA Modules:
  0.0 825.2 jit_solution(14634982966846317152)
XLA Ops:
  10.2 5.6 collective-permute-start
  19.6 30.1 %all_sum.6 = f32[8,512]{1,0:T(8,128)S(1)} custom-call(f32[8,512]{1,0:T(8,128)S(1)} %maximum_maximum_fusion.x_ref), custom_call_target="tpu_custom_call" | custom-call | tf_op jit(solution)/shard_map/all_sum/pallas_call | solution.py:337
  51.7 2.6 fusion.65
  55.3 3.3 collective-permute-start.2
  62.0 1.9 fusion
  64.9 40.0 %collective-permute-done.2.top = f32[13,40,512]{2,1,0:T(8,128)S(1)} collective-permute-done((f32[13,40,512]{2,1,0:T(8,128)S(1)}, f32[13,40,512]{2,1,0:T(8,128)S(1)}, u32[]{:S(2)}, u32[]{:S(2)}) %collective-permute-start.2) | collective-permute-done | bytes 1064992 | tf_op jit(solution)/shard_map/ppermute | solution.py:360
  104.9 15.1 %collective-permute-done.3.bottom = f32[13,40,512]{2,1,0:T(8,128)S(1)} collective-permute-done((f32[13,40,512]{2,1,0:T(8,128)S(1)}, f32[13,40,512]{2,1,0:T(8,128)S(1)}, u32[]{:S(2)}, u32[]{:S(2)}) %collective-permute-start.3) | collective-permute-done | bytes 1064992 | tf_op jit(solution)/shard_map/ppermute | solution.py:361
  121.2 23.6 %conv_forward.1 = (f32[16,40,512]{2,1,0:T(8,128)}, f32[42,80,512]{2,1,0:T(8,128)}, f32[28,80,512]{2,1,0:T(8,128)}, f32[8,512]{1,0:T(8,128)}) custom-call(s32[4,16]{1,0:T(4,128)} %pad_add_fusion.3.bounds, f32[13,40,512]{2,1,0:T(8,128)} %copy-done.50, f32[16,40,512]{2,1,0:T(8,128)} %bitcast.154, f32[13,40,512]{2,1,0:T(8,128)} %copy-done.51, ...), custom_call_target="tpu_custom_call" | custom-call | tf_op jit(solution)/shard_map/conv_forward/pallas_call | solution.py:222
  145.5 35.8 %all_sum.7 = f32[8,512]{1,0:T(8,128)S(1)} custom-call(f32[8,512]{1,0:T(8,128)S(1)} %copy-done.1), custom_call_target="tpu_custom_call" | custom-call | tf_op jit(solution)/shard_map/all_sum/pallas_call | solution.py:337
  182.0 1.7 add_multiply_fusion.6
  185.4 31.0 %all_sum.8 = f32[8,512]{1,0:T(8,128)S(1)} custom-call(f32[8,512]{1,0:T(8,128)S(1)} %maximum_maximum_fusion.1.x_ref), custom_call_target="tpu_custom_call" | custom-call | tf_op jit(solution)/shard_map/all_sum/pallas_call | solution.py:337
  217.1 2.7 fusion.70
  220.8 2.9 convolution_bitcast_fusion
  225.1 2.6 convolution_bitcast_fusion.1
  229.1 2.6 convolution_bitcast_fusion.2
  234.2 2.6 convolution_bitcast_fusion.3
  236.8 4.4 convolution_multiply_fusion.2
  243.4 1.8 convolution_multiply_fusion.3
  247.0 1.8 convolution_multiply_fusion.4
  250.7 1.8 convolution_multiply_fusion.5
  253.6 1.8 convolution_bitcast_fusion.7
  256.4 4.3 pad_maximum_fusion
  260.8 3.0 fusion.88
  263.8 2.7 convolution_add_fusion.2
  269.9 29.5 %all_sum.9 = f32[8,512]{1,0:T(8,128)S(1)} custom-call(f32[8,512]{1,0:T(8,128)S(1)} %maximum_maximum_fusion.2.x_ref), custom_call_target="tpu_custom_call" | custom-call | tf_op jit(solution)/shard_map/all_sum/pallas_call | solution.py:337
  304.0 2.1 fusion.159
  306.2 30.2 %all_sum.10 = f32[8,512]{1,0:T(8,128)S(1)} custom-call(f32[8,512]{1,0:T(8,128)S(1)} %maximum_maximum_fusion.3.x_ref), custom_call_target="tpu_custom_call" | custom-call | tf_op jit(solution)/shard_map/all_sum/pallas_call | solution.py:337
  339.8 6.8 collective-permute-start.4
  348.7 3.9 fusion.83
  352.6 2.6 fusion.96
  355.2 37.2 %collective-permute-done.4.top = f32[13,40,512]{2,1,0:T(8,128)} collective-permute-done((f32[13,40,512]{2,1,0:T(8,128)}, f32[13,40,512]{2,1,0:T(8,128)}, u32[]{:S(2)}, u32[]{:S(2)}) %collective-permute-start.4) | collective-permute-done | bytes 1064992 | tf_op jit(solution)/shard_map/ppermute | solution.py:360
  392.4 25.6 %collective-permute-done.5.bottom = f32[13,40,512]{2,1,0:T(8,128)} collective-permute-done((f32[13,40,512]{2,1,0:T(8,128)}, f32[13,40,512]{2,1,0:T(8,128)}, u32[]{:S(2)}, u32[]{:S(2)}) %collective-permute-start.5) | collective-permute-done | bytes 1064992 | tf_op jit(solution)/shard_map/ppermute | solution.py:361
  418.1 35.2 %conv_backward.1 = (f32[16,40,512]{2,1,0:T(8,128)}, f32[28,32,512]{2,1,0:T(8,128)}) custom-call(s32[4,16]{1,0:T(4,128)} %pad_add_fusion.3.bounds, f32[13,40,512]{2,1,0:T(8,128)} %collective-permute-done.4.top, f32[16,40,512]{2,1,0:T(8,128)} %bitcast.153, f32[13,40,512]{2,1,0:T(8,128)} %collective-permute-done.5.bottom, f32[42,80,512]{2,1,0:T(8,128)} %get-tuple-element.22.xf, ...), custom_call_target="tpu_custom_call" | custom-call | tf_op jit(solution)/shard_map/conv_backward/pallas_call | solution.py:265
  453.3 3.1 slice.154
  458.3 2.6 fusion.66
  461.2 3.6 convolution_add_fusion.5
  464.8 2.8 convolution_add_fusion.4
  467.6 2.8 fusion.8
  472.1 2.6 copy.61
  474.7 2.4 fusion.158
  477.1 118.1 %all-reduce.10.cloned.1.call-done = f32[4,2,512,512]{3,2,0,1:T(8,128)} async-done(((f32[4,2,512,512]{3,2,0,1:T(8,128)}), f32[4,2,512,512]{3,2,0,1:T(8,128)}) %all-reduce.10.cloned.1.call-update) | async-done | bytes 8388624
  595.2 3.7 dynamic-slice_bitcast_fusion
  599.0 20.6 %all_sum.11 = f32[8,512]{1,0:T(8,128)S(1)} custom-call(f32[8,512]{1,0:T(8,128)S(1)} %maximum_maximum_fusion.4.x_ref), custom_call_target="tpu_custom_call" | custom-call | tf_op jit(solution)/shard_map/all_sum/pallas_call | solution.py:337
  620.8 2.3 multiply_add_fusion
  624.8 2.6 copy.62
  627.3 119.1 %all-reduce.12.cloned.1.call-done = (f32[512,512]{1,0:T(8,128)}, f32[27,27,512]{2,1,0:T(8,128)}, f32[512,512]{1,0:T(8,128)}) async-done(((f32[512,512]{1,0:T(8,128)}, f32[27,27,512]{2,1,0:T(8,128)}, f32[512,512]{1,0:T(8,128)}), (f32[512,512]{1,0:T(8,128)}, f32[27,27,512]{2,1,0:T(8,128)}, f32[512,512]{1,0:T(8,128)})) %all-reduce.12.cloned.1.call-update) | async-done | bytes 3590160 | tf_op jit(solution)/shard_map/psum | solution.py:561
  747.9 62.6 %all-reduce.8.cloned.1.call-done = f32[2,512,512]{2,1,0:T(8,128)} async-done(((f32[2,512,512]{2,1,0:T(8,128)}), f32[2,512,512]{2,1,0:T(8,128)}) %all-reduce.8.cloned.1.call-update) | async-done | bytes 2097168 | tf_op jit(solution)/shard_map/psum | solution.py:533
  810.5 3.0 slice_bitcast_fusion
  (229 shorter events, 59.2 us)
Async XLA Ops:
  7.2 44.0 %copy-start = (f32[512,512]{1,0:T(8,128)S(1)}, f32[512,512]{1,0:T(8,128)}, u32[]{:S(2)}) copy-start(f32[512,512]{1,0:T(8,128)} %param.25) | copy-start | bytes 3145732
  7.2 9.0 %copy-start.57 = (s32[16,1,44]{2,1,0:T(1,128)S(1)}, s32[16,1,44]{2,1,0:T(1,128)}, u32[]{:S(2)}) copy-start(s32[16,1,44]{2,1,0:T(1,128)} %param.22) | copy-start | bytes 8452
  7.2 10.3 %copy-start.15 = (f32[16,1,44,512]{3,1,2,0:T(1,128)S(1)}, f32[16,1,44,512]{3,1,2,0:T(1,128)}, u32[]{:S(2)}) copy-start(f32[16,1,44,512]{3,1,2,0:T(1,128)} %param.21) | copy-start | bytes 4325380
  7.2 209.8 %all-gather.5.cloned.1.call-start = ((), (), s32[]{:S(2)}) async-start(), calls=%async_computation.1 | async-start | bytes 5242880 | tf_op jit(solution)/shard_map/all_gather | solution.py:408
  8.0 228.8 %all-gather.7.cloned.1.call-start = ((), (), s32[]{:S(2)}) async-start(), calls=%async_computation.2 | async-start | bytes 5242880 | tf_op jit(solution)/shard_map/all_gather | solution.py:409
  8.9 55.1 %collective-permute-start.1 = (s32[13,2]{0,1:T(2,128)S(1)}, s32[13,2]{0,1:T(2,128)S(1)}, u32[]{:S(2)}, u32[]{:S(2)}) collective-permute-start(s32[13,2]{0,1:T(2,128)S(1)} %get-tuple-element.138), channel_id=1, source_target_pairs={{1,0},{2,1},{3,2},{5,4},{6,5},{7,6},{9,8},{10,9},{11,10},{13,12},{... | collective-permute-start | bytes 320 | tf_op jit(solution)/shard_map/ppermute | solution.py:361
  10.2 53.8 %collective-permute-start = (s32[13,2]{0,1:T(2,128)S(1)}, s32[13,2]{0,1:T(2,128)S(1)}, u32[]{:S(2)}, u32[]{:S(2)}) collective-permute-start(s32[13,2]{0,1:T(2,128)S(1)} %get-tuple-element.137), channel_id=1, source_target_pairs={{0,1},{1,2},{2,3},{4,5},{5,6},{6,7},{8,9},{9,10},{10,11},{12,13},{... | collective-permute-start | bytes 320 | tf_op jit(solution)/shard_map/ppermute | solution.py:360
  15.8 579.4 %all-reduce.10.cloned.1.call-start = ((), (), s32[]{:S(2)}) async-start(), calls=%async_computation.3 | async-start | bytes 16777216
  16.2 45.6 %copy-start.58 = (s32[16,40]{1,0:T(8,128)}, s32[16,40]{1,0:T(8,128)S(1)}, u32[]{:S(2)}) copy-start(s32[16,40]{1,0:T(8,128)S(1)} %pad_add_fusion.2) | copy-start | bytes 7684
  17.0 44.8 %copy-start.60 = (s32[16,40]{1,0:T(8,128)}, s32[16,40]{1,0:T(8,128)S(1)}, u32[]{:S(2)}) copy-start(s32[16,40]{1,0:T(8,128)S(1)} %pad_add_fusion.1) | copy-start | bytes 7684
  18.7 165.0 %copy-start.4 = (f32[16,40,512]{2,1,0:T(8,128)}, f32[16,40,512]{2,1,0:T(8,128)S(1)}, u32[]{:S(2)}) copy-start(f32[16,40,512]{2,1,0:T(8,128)S(1)} %get-tuple-element.139) | copy-start | bytes 3932164
  54.3 5.7 copy-start.45
  54.3 5.7 copy-start.64
  55.3 49.6 %collective-permute-start.2 = (f32[13,40,512]{2,1,0:T(8,128)S(1)}, f32[13,40,512]{2,1,0:T(8,128)S(1)}, u32[]{:S(2)}, u32[]{:S(2)}) collective-permute-start(f32[13,40,512]{2,1,0:T(8,128)S(1)} %bitcast.168), channel_id=1, source_target_pairs={{0,1},{1,2},{2,3},{4,5},{5,6},{6,7},{8,9},{9,10},{10,11},{12,13},{... | collective-permute-start | bytes 3194888 | tf_op jit(solution)/shard_map/ppermute | solution.py:360
  58.7 61.3 %collective-permute-start.3 = (f32[13,40,512]{2,1,0:T(8,128)S(1)}, f32[13,40,512]{2,1,0:T(8,128)S(1)}, u32[]{:S(2)}, u32[]{:S(2)}) collective-permute-start(f32[13,40,512]{2,1,0:T(8,128)S(1)} %bitcast.167), channel_id=1, source_target_pairs={{1,0},{2,1},{3,2},{5,4},{6,5},{7,6},{9,8},{10,9},{11,10},{13,12},{... | collective-permute-start | bytes 3194888 | tf_op jit(solution)/shard_map/ppermute | solution.py:361
  104.9 16.2 %copy-start.50 = (f32[13,40,512]{2,1,0:T(8,128)}, f32[13,40,512]{2,1,0:T(8,128)S(1)}, u32[]{:S(2)}) copy-start(f32[13,40,512]{2,1,0:T(8,128)S(1)} %collective-permute-done.2.top) | copy-start | bytes 3194884
  121.2 60.8 %copy-start.67 = (f32[512]{0:T(512)S(1)}, f32[512]{0:T(512)}, u32[]{:S(2)}) copy-start(f32[512]{0:T(512)} %param.28) | copy-start | bytes 6148
  121.2 60.8 %copy-start.68 = (f32[512]{0:T(512)S(1)}, f32[512]{0:T(512)}, u32[]{:S(2)}) copy-start(f32[512]{0:T(512)} %param.29) | copy-start | bytes 6148
  183.7 33.3 %copy-start.62 = (f32[512]{0:T(512)S(1)}, f32[512]{0:T(512)}, u32[]{:S(2)}) copy-start(f32[512]{0:T(512)} %param.31) | copy-start | bytes 6148
  183.7 33.3 %copy-start.63 = (f32[512]{0:T(512)S(1)}, f32[512]{0:T(512)}, u32[]{:S(2)}) copy-start(f32[512]{0:T(512)} %param.32) | copy-start | bytes 6148
  217.1 6.7 copy-start.9
  236.8 6.1 copy-start.43
  260.7 485.7 %all-reduce.12.cloned.1.call-start = ((), (), s32[]{:S(2)}) async-start(), calls=%async_computation.4 | async-start | bytes 7733248 | tf_op jit(solution)/shard_map/psum | solution.py:561
  260.8 3.0 copy-start.40
  260.8 5.7 copy-start.38
  263.8 3.3 copy-start.10
  268.4 32.3 %copy-start.5 = (f32[16,40,512]{2,1,0:T(8,128)S(1)}, f32[16,40,512]{2,1,0:T(8,128)}, u32[]{:S(2)}) copy-start(f32[16,40,512]{2,1,0:T(8,128)} %copy-done.4) | copy-start | bytes 3932164
  300.7 2.9 copy-start.33
  300.7 3.3 copy-start.70
  302.2 3.9 copy-start.13
  338.0 10.1 %copy-start.71 = (u32[32]{0:T(128)S(1)}, u32[32]{0:T(128)}, u32[]{:S(2)}) copy-start(u32[32]{0:T(128)} %constant.66) | copy-start | bytes 388
  338.1 10.7 %copy-start.48 = (f32[640,512]{1,0:T(8,128)S(1)}, f32[640,512]{1,0:T(8,128)}, u32[]{:S(2)}) copy-start(f32[640,512]{1,0:T(8,128)} %copy-done.46) | copy-start | bytes 3932164
  339.8 52.6 %collective-permute-start.4 = (f32[13,40,512]{2,1,0:T(8,128)}, f32[13,40,512]{2,1,0:T(8,128)}, u32[]{:S(2)}, u32[]{:S(2)}) collective-permute-start(f32[13,40,512]{2,1,0:T(8,128)} %bitcast.44), channel_id=1, source_target_pairs={{0,1},{1,2},{2,3},{4,5},{5,6},{6,7},{8,9},{9,10},{10,11},{12,13},{... | collective-permute-start | bytes 3194888 | tf_op jit(solution)/shard_map/ppermute | solution.py:360
  346.6 71.5 %collective-permute-start.5 = (f32[13,40,512]{2,1,0:T(8,128)}, f32[13,40,512]{2,1,0:T(8,128)}, u32[]{:S(2)}, u32[]{:S(2)}) collective-permute-start(f32[13,40,512]{2,1,0:T(8,128)} %bitcast.46), channel_id=1, source_target_pairs={{1,0},{2,1},{3,2},{5,4},{6,5},{7,6},{9,8},{10,9},{11,10},{13,12},{... | collective-permute-start | bytes 3194888 | tf_op jit(solution)/shard_map/ppermute | solution.py:361
  348.7 3.9 copy-start.14
  348.7 3.9 copy-start.24
  348.7 3.9 copy-start.34
  453.3 3.1 copy-start.41
  453.3 3.1 copy-start.49
  460.9 349.7 %all-reduce.8.cloned.1.call-start = ((), (), s32[]{:S(2)}) async-start(), calls=%async_computation | async-start | bytes 4194304 | tf_op jit(solution)/shard_map/psum | solution.py:533
  461.2 3.6 copy-start.29
  464.8 2.8 copy-start.26
  464.8 2.8 copy-start.42
  467.6 2.8 copy-start.16
  467.6 2.8 copy-start.59
  467.6 2.8 copy-start.61
  598.9 21.9 %copy-start.6 = (f32[16,40,512]{2,1,0:T(8,128)S(1)}, f32[16,40,512]{2,1,0:T(8,128)}, u32[]{:S(2)}) copy-start(f32[16,40,512]{2,1,0:T(8,128)} %copy-done.4) | copy-start | bytes 3932164
  747.9 65.6 %copy-start.53 = (f32[512,512]{1,0:T(8,128)S(1)}, f32[512,512]{1,0:T(8,128)}, u32[]{:S(2)}) copy-start(f32[512,512]{1,0:T(8,128)} %get-tuple-element.154) | copy-start | bytes 3145732
  (35 other events, 58.3 us)
Sparse Core Ops, SparseCore 0:
  9.6 116.2 all-gather.4
  127.5 102.1 all-gather.6
  260.8 334.3 all-reduce.9
  602.2 144.1 all-reduce.11
  749.8 60.6 all-reduce.7

commit v2 on v1

--- a/solution.py
+++ b/solution.py
@@ -24,6 +24,7 @@
 REACH = 13
 SPAN = 2 * REACH + 1
 SPAN_PAD = 32
+LANES = 128
 
 
 def forward_transform(length, padded, positions, columns):
@@ -103,19 +104,11 @@
 GROUP_GRAD = 4
 
 
-def transform_window(rows, window, to_freq_ref, out_ref):
-    for first in range(0, rows, GROUP_IN):
-        part = window[first * SLOTS : (first + GROUP_IN) * SLOTS, :]
+def transform_window(window, to_freq_ref, out_ref):
+    for first in range(0, window.shape[0], GROUP_IN):
+        part = window[first : first + GROUP_IN].reshape(GROUP_IN * SLOTS, window.shape[-1])
         freq = product_split(to_freq_ref, part)
         out_ref[first : first + GROUP_IN] = freq.reshape(GROUP_IN, FREQ, freq.shape[-1])
-
-
-def fill_window(window, top_ref, own_ref, bottom_ref):
-    at = 0
-    for ref in (top_ref, own_ref, bottom_ref):
-        rows = ref.shape[0]
-        window[at : at + rows * SLOTS, :] = ref[...].reshape(rows * SLOTS, ref.shape[-1])
-        at += rows * SLOTS
 
 
 def sum_rows(bounds, rows, x_ref, k_ref, y_ref, flipped, conjugate):
@@ -150,11 +143,10 @@
 
 
 def conv_forward_kernel(
-    bounds, top, own, bottom, taps, mask, to_freq, taps_freq, to_slots, out, xf, kf, stats, window, yf
+    bounds, window, taps, mask, to_freq, taps_freq, to_slots, out, xf, kf, stats, yf
 ):
-    rows = own.shape[0]
-    fill_window(window, top, own, bottom)
-    transform_window(rows + 2 * REACH, window, to_freq, xf)
+    rows = out.shape[0]
+    transform_window(window, to_freq, xf)
     for first in range(0, kf.shape[0], GROUP_TAP):
         part = taps[first : first + GROUP_TAP].reshape(GROUP_TAP * SPAN_PAD, taps.shape[-1])
         freq = product_split(taps_freq, part)
@@ -168,12 +160,11 @@
 
 
 def conv_backward_kernel(
-    bounds, top, own, bottom, xf, kf, mask, to_freq, to_slots, to_taps, out, grad, window, df, yf, gf
+    bounds, window, xf, kf, mask, to_freq, to_slots, to_taps, out, grad, df, yf, gf
 ):
-    rows = own.shape[0]
-    width = own.shape[-1]
-    fill_window(window, top, own, bottom)
-    transform_window(rows + 2 * REACH, window, to_freq, df)
+    rows = out.shape[0]
+    width = out.shape[-1]
+    transform_window(window, to_freq, df)
     sum_rows(bounds, rows, df, kf, yf, True, False)
     rows_to_slots(rows, yf, to_slots, mask, out)
     gf[...] = jnp.zeros(gf.shape, F32)
@@ -211,9 +202,9 @@
     return pl.BlockSpec(array.shape, lambda c, *_: (0,) * array.ndim)
 
 
-def conv_forward(bounds, top, own, bottom, taps, mask):
-    rows, _, channels = own.shape
-    window = rows + 2 * REACH
+def conv_forward(bounds, field, taps, mask):
+    window, _, channels = field.shape
+    rows = window - 2 * REACH
     constants = [
         jnp.asarray(split_constant(slots_to_freq(), GROUP_IN)),
         jnp.asarray(split_constant(taps_to_freq(), GROUP_TAP)),
@@ -225,9 +216,7 @@
             num_scalar_prefetch=1,
             grid=(channels // CHUNK,),
             in_specs=[
-                chunked((REACH, SLOTS)),
-                chunked((rows, SLOTS)),
-                chunked((REACH, SLOTS)),
+                chunked((window, SLOTS)),
                 chunked((TAP_ROWS, SPAN_PAD)),
                 pl.BlockSpec((rows, SLOTS, CHUNK), lambda c, *_: (0, 0, 0)),
             ]
@@ -239,7 +228,6 @@
                 chunked((8,)),
             ],
             scratch_shapes=[
-                pltpu.VMEM((window * SLOTS, CHUNK), F32),
                 pltpu.VMEM((rows, FREQ, CHUNK), F32),
             ],
         ),
@@ -251,12 +239,12 @@
         ],
         compiler_params=pltpu.CompilerParams(vmem_limit_bytes=56 << 20),
         name="conv_forward",
-    )(bounds, top, own, bottom, taps, mask, *constants)
-
-
-def conv_backward(bounds, top, own, bottom, xf, kf, mask):
-    rows, _, channels = own.shape
-    window = rows + 2 * REACH
+    )(bounds, field, taps, mask, *constants)
+
+
+def conv_backward(bounds, field, xf, kf, mask):
+    window, _, channels = field.shape
+    rows = window - 2 * REACH
     constants = [
         jnp.asarray(split_constant(slots_to_freq(), GROUP_IN)),
         jnp.asarray(split_constant(freq_to_slots(), GROUP_OUT)),
@@ -268,9 +256,7 @@
             num_scalar_prefetch=1,
             grid=(channels // CHUNK,),
             in_specs=[
-                chunked((REACH, SLOTS)),
-                chunked((rows, SLOTS)),
-                chunked((REACH, SLOTS)),
+                chunked((window, SLOTS)),
                 chunked((window, FREQ)),
                 chunked((TAP_ROWS, FREQ)),
                 pl.BlockSpec((rows, SLOTS, CHUNK), lambda c, *_: (0, 0, 0)),
@@ -278,7 +264,6 @@
             + [whole(c) for c in constants],
             out_specs=[chunked((rows, SLOTS)), chunked((TAP_ROWS, SPAN_PAD))],
             scratch_shapes=[
-                pltpu.VMEM((window * SLOTS, CHUNK), F32),
                 pltpu.VMEM((window, FREQ, CHUNK), F32),
                 pltpu.VMEM((rows, FREQ, CHUNK), F32),
                 pltpu.VMEM((TAP_ROWS, FREQ, CHUNK), F32),
@@ -290,75 +275,551 @@
         ],
         compiler_params=pltpu.CompilerParams(vmem_limit_bytes=56 << 20),
         name="conv_backward",
-    )(bounds, top, own, bottom, xf, kf, mask, *constants)
-
-
-def all_sum_kernel(dp, rows, x_ref, out_ref, slots, own_sem, send_sem, recv_sem):
-    count = dp * rows
-    me = lax.axis_index("dp") * rows + lax.axis_index("rows")
-    barrier = pltpu.get_barrier_semaphore()
-
-    def place(step):
-        other = lax.rem(me + step, count)
-        return (other // rows, lax.rem(other, rows))
-
-    def greet(step, carry):
-        pl.semaphore_signal(barrier, inc=1, device_id=place(step), device_id_type=MESH)
+    )(bounds, field, xf, kf, mask, *constants)
+
+
+class Net:
+    def __init__(self, dp, rows, send_sem, recv_sem):
+        self.count, self.rows = dp, rows
+        self.send_sem, self.recv_sem, self.used = send_sem, recv_sem, 0
+        self.dp = lax.axis_index("dp")
+        self.z = lax.axis_index("rows")
+        self.bits = list(range(1, dp.bit_length() - 1))
+
+    def bit(self, index):
+        return lax.rem(self.dp // (1 << index), 2)
+
+    def across(self, index):
+        return (self.dp + (1 << index) * (1 - 2 * self.bit(index)), self.z)
+
+    def line(self, step):
+        return (self.dp, lax.rem(self.z + step, self.rows))
+
+    def layer(self, step):
+        return (lax.rem(self.dp + step, self.count), self.z)
+
+    def greet(self):
+        barrier = pltpu.get_barrier_semaphore()
+
+        def greet_line(step, carry):
+            pl.semaphore_signal(barrier, inc=1, device_id=self.line(step), device_id_type=MESH)
+            return carry
+
+        def greet_layer(step, carry):
+            pl.semaphore_signal(barrier, inc=1, device_id=self.layer(step), device_id_type=MESH)
+            return carry
+
+        lax.fori_loop(1, self.rows, greet_line, 0)
+        lax.fori_loop(1, self.count, greet_layer, 0)
+
+    def ready(self):
+        pl.semaphore_wait(pltpu.get_barrier_semaphore(), self.rows + self.count - 2)
+
+    def copy(self, src, dst, device):
+        made = pltpu.make_async_remote_copy(
+            src_ref=src,
+            dst_ref=dst,
+            send_sem=self.send_sem.at[self.used],
+            recv_sem=self.recv_sem.at[self.used],
+            device_id=device,
+            device_id_type=MESH,
+        )
+        self.used += 1
+        return made
+
+    def own(self, src, dst):
+        made = pltpu.make_async_copy(src, dst, self.recv_sem.at[self.used])
+        self.used += 1
+        return made
+
+
+def all_sum_job(net, value, out, line_slots, part, layer_slots):
+    own = net.own(value, line_slots.at[net.z])
+    own.start()
+    sent = [net.copy(value, line_slots.at[net.z], net.line(s)) for s in range(1, net.rows)]
+    for one in sent:
+        one.start()
+    yield
+    own.wait()
+    for one in sent:
+        one.wait()
+    total = line_slots[0]
+    for index in range(1, net.rows):
+        total = total + line_slots[index]
+    part[...] = total
+    own = net.own(part, layer_slots.at[net.dp])
+    own.start()
+    sent = [net.copy(part, layer_slots.at[net.dp], net.layer(s)) for s in range(1, net.count)]
+    for one in sent:
+        one.start()
+    yield
+    own.wait()
+    for one in sent:
+        one.wait()
+    total = layer_slots[0]
+    for index in range(1, net.count):
+        total = total + layer_slots[index]
+    out[...] = total
+
+
+def aligned(value, unit):
+    return pl.multiple_of(value, unit)
+
+
+def halving(net, order, rows):
+    base, steps = 0, []
+    for bit in order:
+        steps.append((bit, base, rows))
+        rows //= 2
+        base = base + net.bit(bit) * rows
+    return steps, base, rows
+
+
+def add_rows(dst, src, count, step):
+    def one(i, carry):
+        at = aligned(i * step, step)
+        to, of = dst(at), src(at)
+        to[...] = to[...] + of[...]
         return carry
 
-    lax.fori_loop(1, count, greet, 0)
-    own = pltpu.make_async_copy(x_ref, slots.at[me], own_sem)
+    lax.fori_loop(0, count // step, one, 0)
+
+
+def run(*jobs):
+    jobs = list(jobs)
+    while jobs:
+        jobs = [job for job in jobs if next(job, StopIteration) is not StopIteration]
+
+
+def line_gather_job(net, value, out):
+    own = net.own(value, out.at[net.z])
     own.start()
-    pl.semaphore_wait(barrier, count - 1)
-
-    def send(step, carry):
-        pltpu.make_async_remote_copy(
-            src_ref=x_ref,
-            dst_ref=slots.at[me],
-            send_sem=send_sem,
-            recv_sem=recv_sem,
-            device_id=place(step),
-            device_id_type=MESH,
-        ).start()
-        return carry
-
-    lax.fori_loop(1, count, send, 0)
+    sent = [net.copy(value, out.at[net.z], net.line(s)) for s in range(1, net.rows)]
+    for one in sent:
+        one.start()
+    yield
     own.wait()
-    others = slots.at[pl.ds(0, count - 1)]
-    pltpu.make_async_copy(others, others, recv_sem).wait()
-    pltpu.make_async_copy(others, others, send_sem).wait()
-    total = slots[0]
-    for index in range(1, count):
-        total = total + slots[index]
-    out_ref[...] = total
-
-
-def all_sum(value, dp, rows, collective_id):
+    for one in sent:
+        one.wait()
+
+
+def sides(net, rows):
+    core = net.bit(0)
+    return [
+        (pl.ds(aligned((2 * core + side) * LANES, LANES), LANES), *halving(net, order, rows))
+        for side, order in enumerate((net.bits, net.bits[::-1]))
+    ]
+
+
+def weights_line_job(net, up, down, wall):
+    own = [net.own(up, wall.at[net.z, 0]), net.own(down, wall.at[net.z, 1])]
+    for one in own:
+        one.start()
+    for one in own:
+        one.wait()
+    last = net.rows - 1
+    for step in range(1, net.rows):
+        moves = []
+        for lanes, _, base, rows in sides(net, up.shape[0]):
+            for way in (1, -1):
+                shard = net.z - way * (step - 1)
+                going = (net.z >= step - 1) & (net.z < last) if way > 0 else (net.z <= last - (step - 1)) & (net.z > 0)
+                coming = net.z >= step if way > 0 else net.z <= last - step
+                shard = lax.rem(shard + net.rows, net.rows)
+                piece = wall.at[shard, :, pl.ds(aligned(base, 8), rows), lanes]
+                one = net.copy(piece, piece, net.line(way % net.rows))
+                pl.when(going)(one.start)
+                moves.append((one, going, coming))
+        yield
+        for one, going, coming in moves:
+            pl.when(coming)(one.wait_recv)
+            pl.when(going)(one.wait_send)
+
+
+def weights_layer_job(net, wall):
+    parts = sides(net, wall.shape[2])
+    for back in range(1, len(net.bits) + 1):
+        moves = []
+        for lanes, steps, _, _ in parts:
+            bit, base, rows = steps[-back]
+            mine = pl.ds(aligned(base + net.bit(bit) * (rows // 2), 8), rows // 2)
+            for step in range(1, net.rows):
+                piece = wall.at[lax.rem(net.z + step, net.rows), :, mine, lanes]
+                moves.append(net.copy(piece, piece, net.across(bit)))
+        for one in moves:
+            one.start()
+        yield
+        for one in moves:
+            one.wait()
+
+
+def weights_pair_job(net, wall):
+    half = wall.shape[3] // 2
+    lanes = pl.ds(aligned(net.bit(0) * half, LANES), half)
+    moves = []
+    for step in range(1, net.rows):
+        piece = wall.at[lax.rem(net.z + step, net.rows), :, :, lanes]
+        moves.append(net.copy(piece, piece, net.across(0)))
+    for one in moves:
+        one.start()
+    yield
+    for one in moves:
+        one.wait()
+
+
+def halo_job(net, field, window, zeros):
+    rows = field.shape[0]
+    own = net.own(field, window.at[pl.ds(REACH, rows)])
+    own.start()
+    has_above, has_below = net.z > 0, net.z < net.rows - 1
+    down = net.copy(field.at[pl.ds(rows - REACH, REACH)], window.at[pl.ds(0, REACH)], net.line(1))
+    up = net.copy(field.at[pl.ds(0, REACH)], window.at[pl.ds(REACH + rows, REACH)], net.line(net.rows - 1))
+    pl.when(has_below)(down.start)
+    pl.when(has_above)(up.start)
+    zeros[...] = jnp.zeros(zeros.shape, F32)
+    top = net.own(zeros, window.at[pl.ds(0, REACH)])
+    bottom = net.own(zeros, window.at[pl.ds(REACH + rows, REACH)])
+    pl.when(jnp.logical_not(has_above))(top.start)
+    pl.when(jnp.logical_not(has_below))(bottom.start)
+    yield
+    own.wait()
+    pl.when(jnp.logical_not(has_above))(top.wait)
+    pl.when(jnp.logical_not(has_below))(bottom.wait)
+    pl.when(has_above)(down.wait_recv)
+    pl.when(has_below)(down.wait_send)
+    pl.when(has_below)(up.wait_recv)
+    pl.when(has_above)(up.wait_send)
+
+
+def reduce_layer_job(net, source, acc, got_pair, got, out):
+    lead, rows, width = source.shape
+    half = width // 2
+    core = net.bit(0)
+    mine = pl.ds(aligned(core * half, LANES), half)
+    other = pl.ds(aligned((1 - core) * half, LANES), half)
+    own = [net.own(source.at[k, :, mine], acc.at[k]) for k in range(lead)]
+    sent = [net.copy(source.at[k, :, other], got_pair.at[k], net.across(0)) for k in range(lead)]
+    for one in own + sent:
+        one.start()
+    yield
+    for k in range(lead):
+        own[k].wait()
+        sent[k].wait()
+        add_rows(lambda at: acc.at[k, pl.ds(at, 32)], lambda at: got_pair.at[k, pl.ds(at, 32)], rows, 32)
+    parts = sides(net, rows)
+    for index in range(len(net.bits)):
+        moves = []
+        for side, (_, steps, _, _) in enumerate(parts):
+            bit, base, size = steps[index]
+            size //= 2
+            give = base + (1 - net.bit(bit)) * size
+            keep = base + net.bit(bit) * size
+            lanes = pl.ds(side * LANES, LANES)
+            place = got.at[side, :, pl.ds(rows - 2 * size, size)]
+            one = net.copy(acc.at[:, pl.ds(aligned(give, 8), size), lanes], place, net.across(bit))
+            one.start()
+            moves.append((one, keep, size, lanes, side))
+        yield
+        for one, keep, size, lanes, side in moves:
+            one.wait()
+            for k in range(lead):
+                add_rows(
+                    lambda at: acc.at[k, pl.ds(aligned(keep + at, 8), 8), lanes],
+                    lambda at: got.at[side, k, pl.ds(rows - 2 * size + at, 8)],
+                    size,
+                    8,
+                )
+    if out is not None:
+        for side, (_, _, base, size) in enumerate(parts):
+            out[side] = acc[:, pl.ds(aligned(base, 8), size), pl.ds(side * LANES, LANES)]
+
+
+def scatter_line_job(net, part, got, out):
+    own = net.own(part.at[:, net.z], got.at[net.z])
+    own.start()
+    sent = []
+    for step in range(1, net.rows):
+        other = lax.rem(net.z + step, net.rows)
+        sent.append(net.copy(part.at[:, other], got.at[net.z], net.line(step)))
+        sent[-1].start()
+    yield
+    own.wait()
+    for one in sent:
+        one.wait()
+    total = got[0]
+    for index in range(1, net.rows):
+        total = total + got[index]
+    out[...] = total
+
+
+def gather_layer_job(net, out):
+    parts = sides(net, out.shape[0])
+    for back in range(1, len(net.bits) + 1):
+        moves = []
+        for lanes, steps, _, _ in parts:
+            bit, base, rows = steps[-back]
+            mine = pl.ds(aligned(base + net.bit(bit) * (rows // 2), 8), rows // 2)
+            piece = out.at[mine, lanes]
+            one = net.copy(piece, piece, net.across(bit))
+            one.start()
+            moves.append(one)
+        yield
+        for one in moves:
+            one.wait()
+    half = out.shape[1] // 2
+    piece = out.at[:, pl.ds(aligned(net.bit(0) * half, LANES), half)]
+    one = net.copy(piece, piece, net.across(0))
+    one.start()
+    yield
+    one.wait()
+
+
+def place_then_gather_job(net, part, out):
+    own = []
+    for side, (lanes, _, base, rows) in enumerate(sides(net, out.shape[0])):
+        own.append(net.own(part.at[side], out.at[pl.ds(aligned(base, 8), rows), lanes]))
+        own[-1].start()
+    for one in own:
+        one.wait()
+    yield from gather_layer_job(net, out)
+
+
+def reduce_all_job(net, source, acc, got_pair, got, got_line, out):
+    yield from reduce_layer_job(net, source, acc, got_pair, got, None)
+    parts = sides(net, source.shape[1])
+    moves, own = [], []
+    for side, (_, _, base, rows) in enumerate(parts):
+        rows //= net.rows
+        inner = pl.ds(side * LANES, LANES)
+        own.append(net.own(acc.at[0, pl.ds(aligned(base + net.z * rows, 8), rows), inner], got_line.at[side, net.z]))
+        for step in range(1, net.rows):
+            other = lax.rem(net.z + step, net.rows)
+            piece = acc.at[0, pl.ds(aligned(base + other * rows, 8), rows), inner]
+            moves.append(net.copy(piece, got_line.at[side, net.z], net.line(step)))
+    for one in own + moves:
+        one.start()
+    yield
+    for one in own + moves:
+        one.wait()
+    moves = []
+    for side, (lanes, _, base, rows) in enumerate(parts):
+        rows //= net.rows
+        total = got_line[side, 0]
+        for index in range(1, net.rows):
+            total = total + got_line[side, index]
+        piece = out.at[pl.ds(aligned(base + net.z * rows, 8), rows), lanes]
+        out[pl.ds(aligned(base + net.z * rows, 8), rows), lanes] = total
+        for step in range(1, net.rows):
+            moves.append(net.copy(piece, piece, net.line(step)))
+            moves[-1].start()
+    yield
+    for one in moves:
+        one.wait()
+    yield from gather_layer_job(net, out)
+
+
+VMEM = pl.BlockSpec(memory_space=pltpu.VMEM)
+HBM = pl.BlockSpec(memory_space=pltpu.HBM)
+COPIES = 96
+
+
+def shape(*dims):
+    return jax.ShapeDtypeStruct(dims, F32)
+
+
+def exchange(name, number, mesh, body, args, in_specs, outs, out_specs, scratch, aliases=None):
+    dp, rows = mesh
+
+    def kernel(*refs):
+        *refs, send_sem, recv_sem = refs
+        net = Net(dp, rows, send_sem, recv_sem)
+        net.greet()
+        net.ready()
+        body(net, *refs)
+        assert net.used <= COPIES
+
     return pl.pallas_call(
-        functools.partial(all_sum_kernel, dp, rows),
-        out_shape=jax.ShapeDtypeStruct(value.shape, F32),
-        in_specs=[pl.BlockSpec(memory_space=pltpu.VMEM)],
-        out_specs=pl.BlockSpec(memory_space=pltpu.VMEM),
-        scratch_shapes=[
-            pltpu.VMEM((dp * rows,) + value.shape, F32),
-            pltpu.SemaphoreType.DMA,
-            pltpu.SemaphoreType.DMA,
-            pltpu.SemaphoreType.DMA,
+        kernel,
+        out_shape=outs,
+        in_specs=in_specs,
+        out_specs=out_specs,
+        scratch_shapes=scratch + [pltpu.SemaphoreType.DMA((COPIES,))] * 2,
+        input_output_aliases=aliases or {},
+        compiler_params=pltpu.CompilerParams(
+            collective_id=number, has_side_effects=True, vmem_limit_bytes=48 << 20
+        ),
+        name=name,
+    )(*args)
+
+
+def sum_scratch(mesh, height):
+    dp, rows = mesh
+    return [pltpu.VMEM((rows, height, LANES), F32), pltpu.VMEM((height, LANES), F32), pltpu.VMEM((dp, height, LANES), F32)]
+
+
+def sums_names_weights(mesh, value, names, up, down):
+    rows = mesh[1]
+
+    def body(net, value, names, up, down, total, all_names, wall, *slots):
+        run(
+            all_sum_job(net, value, total, *slots),
+            line_gather_job(net, names, all_names),
+            weights_line_job(net, up, down, wall),
+        )
+
+    return exchange(
+        "sums_one",
+        0,
+        mesh,
+        body,
+        (value, names, up, down),
+        [VMEM, VMEM, HBM, HBM],
+        [
+            shape(*value.shape),
+            jax.ShapeDtypeStruct((rows,) + names.shape, jnp.int32),
+            shape(rows, 2, *up.shape),
         ],
-        compiler_params=pltpu.CompilerParams(
-            collective_id=collective_id, has_side_effects=True, vmem_limit_bytes=32 << 20
-        ),
-        name="all_sum",
-    )(value)
-
-
-def neighbours(cells, width):
-    count = lax.axis_size("rows")
-    down = [(i, i + 1) for i in range(count - 1)]
-    up = [(i + 1, i) for i in range(count - 1)]
-    return (
-        lax.ppermute(cells[-width:], "rows", down),
-        lax.ppermute(cells[:width], "rows", up),
+        [VMEM, VMEM, HBM],
+        sum_scratch(mesh, value.shape[0]),
+    )
+
+
+def halo_weights(mesh, field, wall):
+    rows = field.shape[0]
+
+    def body(net, field, wall_in, window, wall, zeros):
+        run(halo_job(net, field, window, zeros), weights_layer_job(net, wall))
+
+    return exchange(
+        "halo_act",
+        1,
+        mesh,
+        body,
+        (field, wall),
+        [HBM, HBM],
+        [shape(rows + 2 * REACH, *field.shape[1:]), shape(*wall.shape)],
+        [HBM, HBM],
+        [pltpu.VMEM((REACH,) + field.shape[1:], F32)],
+        {1: 1},
+    )
+
+
+def sums_weights(mesh, value, wall):
+    def body(net, value, wall_in, total, wall, *slots):
+        run(all_sum_job(net, value, total, *slots), weights_pair_job(net, wall))
+
+    return exchange(
+        "sums_two",
+        2,
+        mesh,
+        body,
+        (value, wall),
+        [VMEM, HBM],
+        [shape(*value.shape), shape(*wall.shape)],
+        [VMEM, HBM],
+        sum_scratch(mesh, value.shape[0]),
+        {1: 1},
+    )
+
+
+def sums_only(mesh, name, number, value):
+    def body(net, value, total, *slots):
+        run(all_sum_job(net, value, total, *slots))
+
+    return exchange(
+        name, number, mesh, body, (value,), [VMEM], shape(*value.shape), VMEM, sum_scratch(mesh, value.shape[0])
+    )
+
+
+def layer_scratch(lead, rows, width):
+    return [
+        pltpu.VMEM((lead, rows, width // 2), F32),
+        pltpu.VMEM((lead, rows, width // 2), F32),
+        pltpu.VMEM((2, lead, rows, LANES), F32),
+    ]
+
+
+def sums_grads(mesh, value, grads):
+    lead, rows, width = grads.shape
+
+    def body(net, value, grads, total, part, line, mid, layer, acc, got_pair, got):
+        run(
+            all_sum_job(net, value, total, line, mid, layer),
+            reduce_layer_job(net, grads, acc, got_pair, got, part),
+        )
+
+    return exchange(
+        "sums_four",
+        4,
+        mesh,
+        body,
+        (value, grads),
+        [VMEM, HBM],
+        [shape(*value.shape), shape(2, lead, 2 * rows // mesh[0], LANES)],
+        [VMEM, VMEM],
+        sum_scratch(mesh, value.shape[0]) + layer_scratch(lead, rows, width),
+    )
+
+
+def sums_scatter(mesh, value, part):
+    def body(net, value, part, total, mine, line, mid, layer, got):
+        run(all_sum_job(net, value, total, line, mid, layer), scatter_line_job(net, part, got, mine))
+
+    piece = (2,) + part.shape[2:]
+    return exchange(
+        "sums_five",
+        5,
+        mesh,
+        body,
+        (value, part),
+        [VMEM, VMEM],
+        [shape(*value.shape), shape(*piece)],
+        [VMEM, VMEM],
+        sum_scratch(mesh, value.shape[0]) + [pltpu.VMEM((mesh[1],) + piece, F32)],
+    )
+
+
+def halo_grads(mesh, field, part, height, width):
+    rows = field.shape[0]
+
+    def body(net, field, part, window, grads, zeros):
+        run(halo_job(net, field, window, zeros), place_then_gather_job(net, part, grads))
+
+    return exchange(
+        "halo_grad",
+        6,
+        mesh,
+        body,
+        (field, part),
+        [HBM, VMEM],
+        [shape(rows + 2 * REACH, *field.shape[1:]), shape(height, width)],
+        [HBM, VMEM],
+        [pltpu.VMEM((REACH,) + field.shape[1:], F32)],
+    )
+
+
+def sums_all_grads(mesh, value, grads):
+    rows, width = grads.shape
+    piece = 2 * rows // mesh[0] // mesh[1]
+
+    def body(net, value, grads, total, out, line, mid, layer, acc, got_pair, got, got_line):
+        run(
+            all_sum_job(net, value, total, line, mid, layer),
+            reduce_all_job(net, grads, acc, got_pair, got, got_line, out),
+        )
+
+    return exchange(
+        "sums_six",
+        7,
+        mesh,
+        body,
+        (value, grads.reshape(1, rows, width)),
+        [VMEM, HBM],
+        [shape(*value.shape), shape(rows, width)],
+        [VMEM, VMEM],
+        sum_scratch(mesh, value.shape[0])
+        + layer_scratch(1, rows, width)
+        + [pltpu.VMEM((2, mesh[1], piece, LANES), F32)],
     )
 
 
@@ -405,8 +866,7 @@
     assert canvases == 1 and kernel_big.shape[0] == SPAN
     pixels = rows * SLOTS
     ids = image_ids[:, 0]
-    w_up_all = lax.all_gather(w_up, "rows")
-    w_down_all = lax.all_gather(w_down, "rows")
+    mesh = (dp, devices_rows)
 
     place = jnp.arange(columns, dtype=jnp.int32)[None, :]
     is_left = (ids >= 0) & (ids < LEFT_IDS)
@@ -439,10 +899,43 @@
     slot_mask = jnp.max(pick, axis=2)
     valid = (ids >= 0).astype(F32)
 
+    def compact(field):
+        out = lax.dot_general(
+            pick, field[:, 0], (((2,), (1,)), ((0,), (0,))), precision=HIGHEST, preferred_element_type=F32
+        )
+        return out.reshape(pixels, channels)
+
+    def expand(cells):
+        return lax.dot_general(
+            pick,
+            cells.reshape(rows, SLOTS, channels),
+            (((1,), (1,)), ((0,), (0,))),
+            precision=HIGHEST,
+            preferred_element_type=F32,
+        )[:, None]
+
+    def pack(first, second):
+        return jnp.stack([first, second]).reshape(2 * channels // LANES, LANES)
+
+    def sums(field):
+        return jnp.sum(field, axis=0), jnp.sum(field * field, axis=0)
+
     names = jnp.stack([left_id, right_id], axis=1) + 1
-    above, below = neighbours(names, REACH)
-    window_names = jnp.concatenate([above, names, below], axis=0)
+    names_tile = jnp.pad(names.reshape(1, 2 * rows), ((0, 7), (0, LANES - 2 * rows)))
+    x = compact(inputs)
+    gy = compact(out_grad)
+    total, all_names, wall = sums_names_weights(
+        mesh,
+        jnp.concatenate([pack(*sums(x)), pack(jnp.full((channels,), jnp.sum(valid)), jnp.zeros((channels,)))]),
+        names_tile,
+        w_up,
+        w_down,
+    )
+    count = total[8, 0]
+    total = total[:8].reshape(2, channels)
+    all_names = jnp.pad(all_names[:, 0, : 2 * rows].reshape(devices_rows * rows, 2), ((REACH, REACH), (0, 0)))
     window_rows = rows + 2 * REACH
+    window_names = lax.dynamic_slice_in_dim(all_names, lax.axis_index("rows") * rows, window_rows, 0)
     w_index = jnp.arange(window_rows, dtype=jnp.int32)[None, :]
     r_index = jnp.arange(rows, dtype=jnp.int32)[:, None]
     near = (w_index >= r_index) & (w_index <= r_index + 2 * REACH)
@@ -454,38 +947,8 @@
         bounds += [jnp.minimum(low, high), high]
     bounds = jnp.stack(bounds).astype(jnp.int32)
 
-    def compact(field):
-        out = lax.dot_general(
-            pick, field[:, 0], (((2,), (1,)), ((0,), (0,))), precision=HIGHEST, preferred_element_type=F32
-        )
-        return out.reshape(pixels, channels)
-
-    def expand(cells):
-        return lax.dot_general(
-            pick,
-            cells.reshape(rows, SLOTS, channels),
-            (((1,), (1,)), ((0,), (0,))),
-            precision=HIGHEST,
-            preferred_element_type=F32,
-        )[:, None]
-
     mask = slot_mask.reshape(pixels, 1)
     mask_wide = jnp.broadcast_to(slot_mask[:, :, None], (rows, SLOTS, CHUNK))
-
-    def stack_rows(*rows_list):
-        pad = jnp.zeros((8 - len(rows_list), channels), F32)
-        return jnp.concatenate([row.reshape(1, channels) for row in rows_list] + [pad], axis=0)
-
-    x = compact(inputs)
-    gy = compact(out_grad)
-
-    def sums(field):
-        return jnp.sum(field, axis=0), jnp.sum(field * field, axis=0)
-
-    total = all_sum(
-        stack_rows(*sums(x), jnp.full((channels,), jnp.sum(valid))), dp, devices_rows, 0
-    )
-    count = total[2, 0]
 
     def norm_scale(total):
         mean = total[0] / count
@@ -501,18 +964,18 @@
     edge = (small_start, small_start)
     kernel = kernel_big + jnp.pad(kernel_small, (edge, edge, (0, 0)))
     taps = jnp.pad(kernel, ((0, TAP_ROWS - SPAN), (0, SPAN_PAD - SPAN), (0, 0)))
-    act_above, act_below = neighbours(act, REACH)
-    conv, xf, kf, conv_sums = conv_forward(bounds, act_above, act, act_below, taps, mask_wide)
+    act_window, wall = halo_weights(mesh, act, wall)
+    conv, xf, kf, conv_sums = conv_forward(bounds, act_window, taps, mask_wide)
     conv = conv.reshape(pixels, channels)
-    mean_two, inv_two = norm_scale(all_sum(conv_sums, dp, devices_rows, 1))
+    total, wall = sums_weights(mesh, conv_sums[:2].reshape(8, LANES), wall)
+    mean_two, inv_two = norm_scale(total.reshape(2, channels))
     xhat_two = (conv - mean_two) * inv_two
     u2 = (xhat_two * second_norm_gain + second_norm_bias) * mask
     act2, act2_slope = gelu_parts(u2)
     mixed = x + product(act2, point_two)
     mixed_masked = mixed * mask
-    mean_three, inv_three = norm_scale(
-        all_sum(stack_rows(*sums(mixed_masked)), dp, devices_rows, 2)
-    )
+    total = sums_only(mesh, "sums_three", 3, pack(*sums(mixed_masked)))
+    mean_three, inv_three = norm_scale(total.reshape(2, channels))
     xhat_three = (mixed - mean_three) * inv_three
     u3 = (xhat_three * feedforward_norm_gain + feedforward_norm_bias) * mask
 
@@ -520,47 +983,52 @@
     du3 = jnp.zeros((pixels, channels), F32)
     grad_up, grad_down = [], []
     for part in range(devices_rows):
-        up, down = w_up_all[part], w_down_all[part]
+        up, down = wall[part, 0], wall[part, 1]
         hid, slope = gelu_parts(product(u3, up))
         ffn = ffn + product(hid, down)
         dpre = product_t(gy, down) * slope
         du3 = du3 + product_t(dpre, up)
         grad_up.append(contract(u3, dpre))
         grad_down.append(contract(hid, gy))
-    grad_w = lax.psum_scatter(
-        jnp.stack([jnp.stack(grad_up), jnp.stack(grad_down)], axis=1), "rows", scatter_dimension=0, tiled=False
-    )
-    grad_w = lax.psum(grad_w, "dp")
-
-    def norm_back(dy, xhat, inv, gain, number):
+    grads_ffn = jnp.stack([jnp.stack(grad_up), jnp.stack(grad_down)], axis=1)
+    grads_ffn = grads_ffn.reshape(devices_rows, 2 * channels, grads_ffn.shape[-1])
+
+    def back_sums(dy, xhat):
         masked = dy * mask
-        total = all_sum(
-            stack_rows(jnp.sum(masked, axis=0), jnp.sum(masked * xhat, axis=0)), dp, devices_rows, number
-        )
-        grad_bias, grad_gain = total[0], total[1]
+        return masked, pack(jnp.sum(masked, axis=0), jnp.sum(masked * xhat, axis=0))
+
+    def norm_back(masked, total, xhat, inv, gain):
+        grad_bias, grad_gain = total.reshape(2, channels)
         field = mask * gain * inv * (masked - grad_bias / count - xhat * (grad_gain / count))
         return field, grad_gain, grad_bias
 
+    du3, total = back_sums(du3, xhat_three)
+    total, part = sums_grads(mesh, total, grads_ffn)
     back_three, grad_gain_three, grad_bias_three = norm_back(
-        du3, xhat_three, inv_three, feedforward_norm_gain, 3
+        du3, total, xhat_three, inv_three, feedforward_norm_gain
     )
     dmixed = gy + back_three
     grad_point_two = contract(act2, dmixed)
-    du2 = product_t(dmixed, point_two) * act2_slope
-    dconv, grad_gain_two, grad_bias_two = norm_back(du2, xhat_two, inv_two, second_norm_gain, 4)
-    dconv = dconv.reshape(rows, SLOTS, channels)
-    d_above, d_below = neighbours(dconv, REACH)
-    dact, grad_taps = conv_backward(bounds, d_above, dconv, d_below, xf, kf, mask_wide)
+    du2, total = back_sums(product_t(dmixed, point_two) * act2_slope, xhat_two)
+    total, part = sums_scatter(mesh, total, part)
+    dconv, grad_gain_two, grad_bias_two = norm_back(du2, total, xhat_two, inv_two, second_norm_gain)
+    d_window, grad_w = halo_grads(
+        mesh, dconv.reshape(rows, SLOTS, channels), part, grads_ffn.shape[1], grads_ffn.shape[2]
+    )
+    dact, grad_taps = conv_backward(bounds, d_window, xf, kf, mask_wide)
     dh1 = dact.reshape(pixels, channels) * act_slope
     grad_point_one = contract(u1, dh1)
-    du1 = product_t(dh1, point_one)
-    back_one, grad_gain_one, grad_bias_one = norm_back(du1, xhat_one, inv_one, first_norm_gain, 5)
-    grad_cells = back_three + back_one
+    du1, total = back_sums(product_t(dh1, point_one), xhat_one)
+    grads_all = jnp.concatenate(
+        [grad_point_one, grad_point_two, grad_taps[:SPAN, :SPAN].reshape(SPAN * SPAN, channels)]
+    )
+    unit = 4 * dp * devices_rows
+    grads_all = jnp.pad(grads_all, ((0, -grads_all.shape[0] % unit), (0, 0)))
+    total, grads_all = sums_all_grads(mesh, total, grads_all)
+    back_one, grad_gain_one, grad_bias_one = norm_back(du1, total, xhat_one, inv_one, first_norm_gain)
     output = inputs + expand((mixed - x) + ffn)
-    grad_input = out_grad + expand(grad_cells)
-    grad_point_one, grad_point_two, grad_kernel = lax.psum(
-        (grad_point_one, grad_point_two, grad_taps[:SPAN, :SPAN]), ("dp", "rows")
-    )
+    grad_input = out_grad + expand(back_three + back_one)
+    grad_kernel = grads_all[2 * channels : 2 * channels + SPAN * SPAN].reshape(SPAN, SPAN, channels)
     small_end = small_start + kernel_small.shape[0]
     grad_small = grad_kernel[small_start:small_end, small_start:small_end]
     return (
@@ -568,16 +1036,16 @@
         grad_input,
         grad_gain_one,
         grad_bias_one,
-        grad_point_one,
+        grads_all[:channels],
         grad_kernel,
         grad_small,
         grad_gain_two,
         grad_bias_two,
-        grad_point_two,
+        grads_all[channels : 2 * channels],
         grad_gain_three,
         grad_bias_three,
-        grad_w[0],
-        grad_w[1],
+        grad_w[:channels],
+        grad_w[channels:],
     )
 
 

time: 833 us -> 488 us (0.59)
  waiting for transfers between devices: 418 us -> 0 us
  Pallas kernels: 236 us -> 348 us
  starting transfers between devices: 20.2 us -> 0 us
  between operations: 15.3 us -> 1.87 us
  matrix products: 75.8 us -> 66.3 us
    psum x2 -> x0, waiting for transfers between devices: 182 us -> none  [the longest x1 119 us: shards(): lax.psum((grad_point_one, grad_point_two, grad_taps[:SPAN, :SPAN]), ('dp'...]
    unnamed x6 -> x0, waiting for transfers between devices: 119 us -> none
    ppermute x6 -> x0, waiting for transfers between devices: 118 us -> none  [the longest x3 77.2 us: neighbours(): lax.ppermute(cells[-width:], 'rows', down)]
    pallas_call x6 -> x8, Pallas kernels: 177 us -> 289 us  [exchange(): pl.pallas_call(kernel, out_shape=outs, in_specs=in_specs, out_specs=out_s...]
    ppermute x6 -> x0, starting transfers between devices: 19.8 us -> none  [the longest x3 15.7 us: neighbours(): lax.ppermute(cells[-width:], 'rows', down)]
    unnamed x150 -> x80, local copies, waits for them, and re-layouts: 20.5 us -> 12.2 us
  transfers between devices with their start and end apart: 11 -> 0, of which waited for: 7 -> 0; matrix products, arithmetic and copies ran while one was open for 12% -> 0% of each run, Pallas kernels for 29% -> 0%
where the time goes in v2:
time: 488 us; the launch traced here: 479 us
  Pallas kernels  348 us (71%)
  matrix products  66.3 us (14%)
  local copies, waits for them, and re-layouts  36.1 us (7%)
  other arithmetic  26.8 us (5%)
    pallas_call x8, Pallas kernels, exchange(): pl.pallas_call(kernel, out_shape=outs, in_specs=in_specs, out_specs=out_s...  289 us
    pallas_call x1, Pallas kernels, conv_backward(): pl.pallas_call(conv_backward_kernel, grid_spec=pltpu.PrefetchScalarGridSp...  35.5 us
    pallas_call x1, Pallas kernels, conv_forward(): pl.pallas_call(conv_forward_kernel, grid_spec=pltpu.PrefetchScalarGridSpe...  23.3 us
    dot_general x10, matrix products, product(): return jnp.dot(left, right, precision=HIGH, preferred_element_type=F32)  21.2 us
    dot_general x10, matrix products, product_t(): lax.dot_general(left, right, (((1,), (1,)), ((), ())), precision=HIGH, pr...  19 us
    dot_general x10, matrix products, contract(): lax.dot_general(left, right, (((0,), (0,)), ((), ())), precision=HIGH, pr...  18.1 us
    unnamed x80, local copies, waits for them, and re-layouts  12.2 us

profile of v2, /device:TPU:0, one launch (start us, length us, event | category | flops | bytes accessed | tf_op | source)
XLA Modules:
  0.0 478.9 jit_solution(488367530987720531)
XLA Ops:
  6.8 3.5 fusion.1
  11.6 2.1 pad_add_fusion
  13.7 1.6 pad.24.taps
  15.9 30.9 %sums_one.1 = (f32[16,128]{1,0:T(8,128)S(1)}, s32[4,8,128]{2,1,0:T(8,128)S(1)}, f32[4,2,512,512]{3,2,1,0:T(8,128)}) custom-call(f32[16,128]{1,0:T(8,128)S(1)} %pad_maximum_fusion.1.refs_0_, s32[8,128]{1,0:T(8,128)S(1)} %pad.21.refs_1_, f32[512,512]{1,0:T(8,128)S(1)} %copy-done.2, f32[512,512]{1,0:T(8,128)S(1)} %copy-done.3), custom_call_target="tpu_custom_call" | custom-call | tf_op jit(solution)/shard_map/sums_one/pallas_call | solution.py:641
  50.5 2.6 fusion.66
  53.0 44.6 %halo_act.1 = (f32[42,40,512]{2,1,0:T(8,128)S(1)}, f32[4,2,512,512]{3,2,1,0:T(8,128)}) custom-call(f32[16,40,512]{2,1,0:T(8,128)S(1)} %bitcast.207, f32[4,2,512,512]{3,2,1,0:T(8,128)} %get-tuple-element.37.refs_1_), custom_call_target="tpu_custom_call", output_to_operand_aliasing={{1}: (1, {})} | custom-call | tf_op jit(solution)/shard_map/halo_act/pallas_call | solution.py:641
  97.6 1.8 copy-done.1
  99.5 23.3 %conv_forward.1 = (f32[16,40,512]{2,1,0:T(8,128)}, f32[42,80,512]{2,1,0:T(8,128)}, f32[28,80,512]{2,1,0:T(8,128)}, f32[8,512]{1,0:T(8,128)}) custom-call(s32[4,16]{1,0:T(4,128)} %pad_add_fusion.3.bounds, f32[42,40,512]{2,1,0:T(8,128)} %copy-done.1, f32[28,32,512]{2,1,0:T(8,128)} %pad.24.taps, f32[16,40,256]{2,1,0:T(8,128)} %broadcast_in_dim.124.mask, ...), custom_call_target="tpu_custom_call" | custom-call | tf_op jit(solution)/shard_map/conv_forward/pallas_call | solution.py:213
  123.5 13.1 %sums_two.1 = (f32[8,128]{1,0:T(8,128)S(1)}, f32[4,2,512,512]{3,2,1,0:T(8,128)}) custom-call(f32[8,128]{1,0:T(8,128)S(1)} %reshape.300.refs_0_, f32[4,2,512,512]{3,2,1,0:T(8,128)} %get-tuple-element.41.refs_1_), custom_call_target="tpu_custom_call", output_to_operand_aliasing={{1}: (1, {})} | custom-call | tf_op jit(solution)/shard_map/sums_two/pallas_call | solution.py:641
  139.6 1.6 multiply_reduce_fusion.5
  141.2 10.6 %sums_three.1 = f32[8,128]{1,0:T(8,128)S(1)} custom-call(f32[8,128]{1,0:T(8,128)S(1)} %reshape.301.refs_0_), custom_call_target="tpu_custom_call" | custom-call | tf_op jit(solution)/shard_map/sums_three/pallas_call | solution.py:641
  153.2 2.6 fusion.82
  155.9 1.6 convolution_bitcast_fusion.2
  157.5 2.5 fusion.77
  160.0 1.6 convolution_bitcast_fusion.1
  161.6 2.5 fusion.72
  164.2 1.6 convolution_bitcast_fusion
  167.1 1.6 convolution_bitcast_fusion.3
  169.6 1.8 convolution_multiply_fusion.5
  174.3 1.8 convolution_multiply_fusion.4
  176.1 2.5 convolution_add_fusion.4
  178.6 1.8 convolution_multiply_fusion.3
  180.4 1.6 convolution_bitcast_fusion.5
  182.0 1.8 convolution_bitcast_fusion.6
  183.7 1.6 convolution_bitcast_fusion.7
  189.1 1.8 convolution_multiply_fusion.2
  190.9 2.5 fusion.185
  196.6 4.3 copy.59
  200.9 53.1 %sums_four.1 = (f32[8,128]{1,0:T(8,128)S(1)}, f32[2,4,256,128]{3,2,1,0:T(8,128)S(1)}) custom-call(f32[8,128]{1,0:T(8,128)S(1)} %reshape.304.refs_0_, f32[4,1024,512]{2,1,0:T(8,128)} %bitcast.210), custom_call_target="tpu_custom_call" | custom-call | tf_op jit(solution)/shard_map/sums_four/pallas_call | solution.py:641
  257.4 2.7 fusion.9
  260.2 1.7 bitcast_add_fusion.1
  261.9 2.6 copy.61
  264.5 2.6 fusion.113
  267.1 3.2 fusion.184
  270.3 23.5 %sums_five.1 = (f32[8,128]{1,0:T(8,128)S(1)}, f32[2,256,128]{2,1,0:T(8,128)S(1)}) custom-call(f32[8,128]{1,0:T(8,128)S(1)} %reshape.306.refs_0_, f32[2,4,256,128]{3,2,1,0:T(8,128)S(1)} %get-tuple-element.45.refs_1_), custom_call_target="tpu_custom_call" | custom-call | tf_op jit(solution)/shard_map/sums_five/pallas_call | solution.py:641
  295.0 2.1 subtract_multiply_fusion
  297.1 42.4 %halo_grad.1 = (f32[42,40,512]{2,1,0:T(8,128)}, f32[1024,512]{1,0:T(8,128)S(1)}) custom-call(f32[16,40,512]{2,1,0:T(8,128)S(1)} %bitcast.206, f32[2,256,128]{2,1,0:T(8,128)S(1)} %get-tuple-element.47.refs_1_), custom_call_target="tpu_custom_call" | custom-call | tf_op jit(solution)/shard_map/halo_grad/pallas_call | solution.py:641
  339.5 35.5 %conv_backward.1 = (f32[16,40,512]{2,1,0:T(8,128)}, f32[28,32,512]{2,1,0:T(8,128)}) custom-call(s32[4,16]{1,0:T(4,128)} %pad_add_fusion.3.bounds, f32[42,40,512]{2,1,0:T(8,128)} %get-tuple-element.48.window, f32[42,80,512]{2,1,0:T(8,128)} %get-tuple-element.49.xf, f32[28,80,512]{2,1,0:T(8,128)} %get-tuple-element.50.kf, ...), custom_call_target="tpu_custom_call" | custom-call | tf_op jit(solution)/shard_map/conv_backward/pallas_call | solution.py:253
  375.0 2.2 fusion.18
  377.2 2.6 fusion.67
  379.8 2.5 fusion.183
  382.3 2.9 slice.122
  385.2 2.7 reshape.310
  387.9 4.3 fusion.refs_1_
  392.2 71.0 %sums_six.1 = (f32[8,128]{1,0:T(8,128)S(1)}, f32[1792,512]{1,0:T(8,128)S(1)}) custom-call(f32[8,128]{1,0:T(8,128)S(1)} %reshape.309.refs_0_, f32[1,1792,512]{2,1,0:T(8,128)} %fusion.refs_1_), custom_call_target="tpu_custom_call" | custom-call | tf_op jit(solution)/shard_map/sums_six/pallas_call | solution.py:641
  465.8 1.7 bitcast_add_fusion
  467.4 2.6 copy.62
  472.8 2.7 reshape.313
  (152 shorter events, 41.6 us)
Async XLA Ops:
  0.6 49.3 %copy-start = (f32[512,512]{1,0:T(8,128)S(1)}, f32[512,512]{1,0:T(8,128)}, u32[]{:S(2)}) copy-start(f32[512,512]{1,0:T(8,128)} %param.25) | copy-start | bytes 3145732
  6.8 3.5 copy-start.12
  6.8 3.5 copy-start.27
  10.3 1.3 copy-start.30
  11.5 38.3 %copy-start.6 = (f32[16,40,512]{2,1,0:T(8,128)}, f32[16,40,512]{2,1,0:T(8,128)S(1)}, u32[]{:S(2)}) copy-start(f32[16,40,512]{2,1,0:T(8,128)S(1)} %get-tuple-element.148) | copy-start | bytes 3932164
  13.7 1.6 copy-start.2
  13.7 2.2 copy-start.3
  49.8 0.7 copy-start.31
  49.8 0.7 copy-start.32
  50.5 2.6 copy-start.4
  97.6 1.8 copy-start.1
  123.5 14.4 %copy-start.15 = (f32[16,40,512]{2,1,0:T(8,128)S(1)}, f32[16,40,512]{2,1,0:T(8,128)}, u32[]{:S(2)}) copy-start(f32[16,40,512]{2,1,0:T(8,128)} %get-tuple-element.39) | copy-start | bytes 3932164
  123.5 14.4 %copy-start.33 = (f32[512]{0:T(512)S(1)}, f32[512]{0:T(512)}, u32[]{:S(2)}) copy-start(f32[512]{0:T(512)} %param.28) | copy-start | bytes 6148
  123.5 14.4 %copy-start.34 = (f32[512]{0:T(512)S(1)}, f32[512]{0:T(512)}, u32[]{:S(2)}) copy-start(f32[512]{0:T(512)} %param.29) | copy-start | bytes 6148
  137.9 1.3 copy-start.7
  138.0 1.6 copy-start.35
  139.6 1.6 copy-start.19
  139.6 13.6 %copy-start.28 = (f32[512]{0:T(512)S(1)}, f32[512]{0:T(512)}, u32[]{:S(2)}) copy-start(f32[512]{0:T(512)} %param.31) | copy-start | bytes 6148
  139.6 13.6 %copy-start.29 = (f32[512]{0:T(512)S(1)}, f32[512]{0:T(512)}, u32[]{:S(2)}) copy-start(f32[512]{0:T(512)} %param.32) | copy-start | bytes 6148
  153.2 2.6 copy-start.17
  155.8 10.0 %slice-start = ((s8[8388608]{0:T(1024)(128)(4,1)}), s8[4194304]{0:T(1024)(128)(4,1)S(1)}, s32[]{:S(2)}) async-start(s8[8388608]{0:T(1024)(128)(4,1)} %bitcast.208), calls=%async_computation | async-start | bytes 8388608
  160.0 5.8 %slice-start.1 = ((s8[8388608]{0:T(1024)(128)(4,1)}), s8[4194304]{0:T(1024)(128)(4,1)S(1)}, s32[]{:S(2)}) async-start(s8[8388608]{0:T(1024)(128)(4,1)} %bitcast.208), calls=%async_computation.1 | async-start | bytes 8388608
  164.2 24.9 %copy-start.21 = (f32[640,512]{1,0:T(8,128)}, f32[640,512]{1,0:T(8,128)S(1)}, u32[]{:S(2)}) copy-start(f32[640,512]{1,0:T(8,128)S(1)} %fusion.72) | copy-start | bytes 3932164
  200.9 54.3 %copy-start.8 = (f32[16,40,512]{2,1,0:T(8,128)S(1)}, f32[16,40,512]{2,1,0:T(8,128)}, u32[]{:S(2)}) copy-start(f32[16,40,512]{2,1,0:T(8,128)} %copy-done.6) | copy-start | bytes 3932164
  200.9 54.3 %copy-start.25 = (f32[640,512]{1,0:T(8,128)S(1)}, f32[640,512]{1,0:T(8,128)}, u32[]{:S(2)}) copy-start(f32[640,512]{1,0:T(8,128)} %get-tuple-element.152) | copy-start | bytes 3932164
  255.2 1.3 copy-start.22
  255.2 2.2 copy-start.24
  255.7 11.4 %copy-start.10 = (f32[640,512]{1,0:T(8,128)}, f32[640,512]{1,0:T(8,128)S(1)}, u32[]{:S(2)}) copy-start(f32[640,512]{1,0:T(8,128)S(1)} %get-tuple-element.136) | copy-start | bytes 3932164
  257.4 2.8 copy-start.13
  261.8 2.6 copy-start.18
  261.9 2.6 copy-start.20
  264.4 2.6 copy-start.16
  264.5 2.6 copy-start.36
  339.5 35.5 %copy-start.23 = (f32[640,512]{1,0:T(8,128)S(1)}, f32[640,512]{1,0:T(8,128)}, u32[]{:S(2)}) copy-start(f32[640,512]{1,0:T(8,128)} %get-tuple-element.150) | copy-start | bytes 3932164
  375.0 2.2 copy-start.5
  387.9 76.5 %copy-start.26 = (f32[640,512]{1,0:T(8,128)S(1)}, f32[640,512]{1,0:T(8,128)}, u32[]{:S(2)}) copy-start(f32[640,512]{1,0:T(8,128)} %get-tuple-element.154) | copy-start | bytes 3932164
  392.2 72.2 %copy-start.9 = (f32[16,40,512]{2,1,0:T(8,128)S(1)}, f32[16,40,512]{2,1,0:T(8,128)}, u32[]{:S(2)}) copy-start(f32[16,40,512]{2,1,0:T(8,128)} %copy-done.6) | copy-start | bytes 3932164
  392.2 72.2 %copy-start.11 = (f32[640,512]{1,0:T(8,128)S(1)}, f32[640,512]{1,0:T(8,128)}, u32[]{:S(2)}) copy-start(f32[640,512]{1,0:T(8,128)} %copy-done.10) | copy-start | bytes 3932164
  464.4 1.4 copy-start.14
